TPU v7x, 256 devices: a whole 4x4x8 slice. The times are simulated.
256 devices in a mesh: rep: 16 (over y, z_lo), tp: 16 (over z_hi, x, core).
Axes of the slice: x: 4, y: 4, z: 8 (z_hi: 2, z_lo: 4; z = z_hi * 4 + z_lo), core: 2. Of those that a mesh axis runs over, the one named last changes fastest.
Arguments:
- hidden: bfloat16 [4, 256, 8192], P(None, ('rep', 'tp')), may hold values from -6 to 6
- w_query: bfloat16 [8192, 8192], P(None, 'tp'), may hold values from -0.0625 to 0.0625
- w_key: bfloat16 [8192, 512], P(None, 'tp'), may hold values from -0.1875 to 0.1875
- w_value: bfloat16 [8192, 512], P(None, 'tp'), may hold values from -0.0625 to 0.0625
- a_factors: bfloat16 [3, 8192, 64], P(None, 'rep'), may hold values from -0.0625 to 0.0625
- b_query: bfloat16 [64, 8192], P('rep', 'tp'), may hold values from -0.75 to 0.75
- b_key: bfloat16 [64, 512], P('rep', 'tp'), may hold values from -2 to 2
- b_value: bfloat16 [64, 512], P('rep', 'tp'), may hold values from -0.75 to 0.75
- key_cache: bfloat16 [256, 1536, 512], P(('rep', 'tp'))
- value_cache: bfloat16 [256, 1536, 512], P(('rep', 'tp')), may hold values from -6 to 6
- lengths: int32 [256], P(('rep', 'tp')), may hold values from 512 to 1536, as said below
Outputs:
- attended: bfloat16 [4, 256, 8192], P(None, 'rep', 'tp')
- new_keys: bfloat16 [4, 256, 512], P(None, ('rep', 'tp'))
- new_values: bfloat16 [4, 256, 512], P(None, ('rep', 'tp'))
Inputs may be any that keep to these rules, and one draw needn't show every extreme that they name: Row r has its keys and values in slots 0 to lengths[r] - 1; some row has 1536 and some row 512.
All inputs are finite; a program needn't handle non-finite values.
Results may differ from a plain program's by a relative error of at most 0.0085.
The roundings to bfloat16 on the way count: a program that leaves them out, or rounds other values in their place, can miss the bound.
Values may be sent and summed in bfloat16 or wider, within the bound.
A program may use at most 128 MiB of HBM per device.

v0:
```python
import math

import jax
import jax.numpy as jnp
from jax import lax
from jax.sharding import PartitionSpec as P

HEAD_DIM = 128
STEPS = 4


THETA = 500000.0
SCALE = 0.5


def rotate(values, positions):
    half_dim = values.shape[-1] // 2
    frequency = THETA ** (-(jnp.arange(half_dim, dtype=jnp.float32) * 2.0 / values.shape[-1]))
    angles = positions.astype(jnp.float32)[:, None, None] * frequency
    cosine = jnp.cos(angles)
    sine_part = jnp.sin(angles)
    low_half = values[..., :half_dim]
    high_half = values[..., half_dim:]
    return jnp.concatenate(
        [low_half * cosine - high_half * sine_part, high_half * cosine + low_half * sine_part], -1
    )


def attend(query, cache_keys, cache_values, fresh_keys, fresh_values, valid):
    row_count = query.shape[0]
    heads_kv = cache_keys.shape[2]
    scaling = 1.0 / math.sqrt(HEAD_DIM)
    grouped = query.reshape(row_count, heads_kv, -1, HEAD_DIM)
    cache_scores = (
        jnp.einsum("rkgd,rckd->rkgc", grouped, cache_keys, preferred_element_type=jnp.float32)
        * scaling
    )
    fresh_scores = (
        jnp.einsum("rkgd,rskd->rkgs", grouped, fresh_keys, preferred_element_type=jnp.float32)
        * scaling
    )
    in_cache = valid[:, None, None, :]
    cache_scores = jnp.where(in_cache, cache_scores, -1e30)
    highest = jnp.maximum(jnp.max(cache_scores, -1), jnp.max(fresh_scores, -1))[..., None]
    cache_weights = jnp.where(in_cache, jnp.exp(cache_scores - highest), 0.0)
    merged_weights = jnp.exp(fresh_scores - highest)
    denominator = jnp.sum(cache_weights, -1, keepdims=True) + jnp.sum(
        merged_weights, -1, keepdims=True
    )
    cache_probs = (cache_weights / denominator).astype(jnp.bfloat16)
    fresh_probs = (merged_weights / denominator).astype(jnp.bfloat16)
    blended = jnp.einsum(
        "rkgc,rckd->rkgd", cache_probs, cache_values, preferred_element_type=jnp.float32
    )
    blended = blended + jnp.einsum(
        "rkgs,rskd->rkgd", fresh_probs, fresh_values, preferred_element_type=jnp.float32
    )
    return blended.reshape(row_count, -1).astype(jnp.bfloat16)


def shards(
    hidden,
    w_query,
    w_key,
    w_value,
    a_factors,
    b_query,
    b_key,
    b_value,
    key_cache,
    value_cache,
    lengths,
):
    up_query, up_key, up_value = (
        lax.all_gather(b_query, "rep", axis=0, tiled=True),
        lax.all_gather(b_key, "rep", axis=0, tiled=True),
        lax.all_gather(b_value, "rep", axis=0, tiled=True),
    )
    query_cols = w_query.shape[1]
    key_cols = w_key.shape[1]
    piece = lax.all_gather(a_factors, "rep", axis=1, tiled=True)
    merged_parts = []
    for weight, which, upward_factor in (
        (w_query, 0, up_query),
        (w_key, 1, up_key),
        (w_value, 2, up_value),
    ):
        low_rank = jnp.dot(piece[which], upward_factor, preferred_element_type=jnp.float32)
        merged_parts.append((weight.astype(jnp.float32) + SCALE * low_rank).astype(jnp.bfloat16))
    merged = jnp.concatenate(merged_parts, 1)
    own_rows = key_cache.shape[0]
    shaped_keys = key_cache.reshape(own_rows, key_cache.shape[1], -1, HEAD_DIM)
    shaped_values = value_cache.reshape(own_rows, value_cache.shape[1], -1, HEAD_DIM)
    valid = jnp.arange(key_cache.shape[1])[None, :] < lengths[:, None]
    outputs = []
    key_list = []
    value_list = []
    for step_index in range(STEPS):
        projected = jnp.dot(
            lax.all_gather(hidden[step_index], "tp", axis=0, tiled=True),
            merged,
            preferred_element_type=jnp.float32,
        ).astype(jnp.bfloat16)
        own_query, own_key, own_value = (
            lax.all_to_all(
                projected[:, :query_cols], "tp", split_axis=0, concat_axis=1, tiled=True
            ),
            lax.all_to_all(
                projected[:, query_cols : query_cols + key_cols],
                "tp",
                split_axis=0,
                concat_axis=1,
                tiled=True,
            ),
            lax.all_to_all(
                projected[:, query_cols + key_cols :], "tp", split_axis=0, concat_axis=1, tiled=True
            ),
        )
        positions = lengths + step_index
        query = rotate(own_query.astype(jnp.float32).reshape(own_rows, -1, HEAD_DIM), positions)
        query = query.astype(jnp.bfloat16).reshape(own_rows, -1)
        new_key = rotate(
            own_key.astype(jnp.float32).reshape(own_rows, -1, HEAD_DIM), positions
        ).astype(jnp.bfloat16)
        key_list.append(new_key)
        value_list.append(own_value.reshape(own_rows, -1, HEAD_DIM))
        attended = attend(
            query,
            shaped_keys,
            shaped_values,
            jnp.stack(key_list, 1),
            jnp.stack(value_list, 1),
            valid,
        )
        outputs.append(lax.all_to_all(attended, "tp", split_axis=1, concat_axis=0, tiled=True))
    result = jnp.stack(outputs)
    new_keys = jnp.stack(key_list).reshape(STEPS, own_rows, -1)
    new_values = jnp.stack(value_list).reshape(STEPS, own_rows, -1)
    return (result, new_keys, new_values)


def solution(mesh):
    placed = (
        P(None, ("rep", "tp"), None),
        P(None, "tp"),
        P(None, "tp"),
        P(None, "tp"),
        P(None, "rep", None),
        P("rep", "tp"),
        P("rep", "tp"),
        P("rep", "tp"),
        P(("rep", "tp"), None, None),
        P(("rep", "tp"), None, None),
        P(("rep", "tp")),
    )
    return jax.shard_map(
        shards,
        mesh=mesh,
        in_specs=placed,
        out_specs=(
            P(None, "rep", "tp"),
            P(None, ("rep", "tp"), None),
            P(None, ("rep", "tp"), None),
        ),
        check_vma=False,
    )
```

profile of v0, /device:TPU:1, one launch (start us, length us, event | category | flops | bytes accessed | tf_op | source)
XLA Modules:
  0.0 527.1 jit_solution(6765820711627343738)
XLA Ops:
  8.0 11.5 %copy.86 = bf16[8192,512]{0,1:T(8,128)(2,1)} copy(bf16[8192,512]{1,0:T(8,128)(2,1)} %param.12) | data formatting | bytes 16777216 | tf_op args[1]
  19.5 40.2 %all-gather.4 = bf16[16,4,512]{2,1,0:T(4,128)(2,1)S(1)} all-gather(bf16[1,4,512]{2,1,0:T(4,128)(2,1)S(1)} %bitcast.203), channel_id=1, replica_groups=mesh['rep'=16,'tp'=16] {'rep'}, dimensions={0}, use_global_device_ids=true | all-gather | bytes 69632 | tf_op jit(solution)/shard_map/all_gather | solution.py:75
  63.1 31.1 %all-gather.5 = bf16[16,4,32]{2,1,0:T(4,128)(2,1)S(1)} all-gather(bf16[1,4,32]{2,1,0:T(4,128)(2,1)S(1)} %bitcast.204), channel_id=1, replica_groups=mesh['rep'=16,'tp'=16] {'rep'}, dimensions={0}, use_global_device_ids=true | all-gather | bytes 4352 | tf_op jit(solution)/shard_map/all_gather | solution.py:76
  94.3 32.6 %all-gather.6 = bf16[16,4,32]{2,1,0:T(4,128)(2,1)S(1)} all-gather(bf16[1,4,32]{2,1,0:T(4,128)(2,1)S(1)} %bitcast.205), channel_id=1, replica_groups=mesh['rep'=16,'tp'=16] {'rep'}, dimensions={0}, use_global_device_ids=true | all-gather | bytes 4352 | tf_op jit(solution)/shard_map/all_gather | solution.py:77
  127.3 51.3 %all-gather = bf16[16,1,8192]{2,1,0:T(2,128)(2,1)} all-gather(bf16[1,1,8192]{2,1,0:T(2,128)(2,1)S(1)} %get-tuple-element.19), channel_id=2, replica_groups=mesh['rep'=16,'tp'=16] {'tp'}, dimensions={0}, use_global_device_ids=true | all-gather | bytes 278528 | tf_op jit(solution)/shard_map/all_gather | solution.py:100
  178.6 26.9 %all-gather.1 = bf16[16,1,8192]{2,1,0:T(2,128)(2,1)} all-gather(bf16[1,1,8192]{2,1,0:T(2,128)(2,1)S(1)} %get-tuple-element.18), channel_id=3, replica_groups=mesh['rep'=16,'tp'=16] {'tp'}, dimensions={0}, use_global_device_ids=true | all-gather | bytes 278528 | tf_op jit(solution)/shard_map/all_gather | solution.py:100
  205.5 28.2 %all-gather.3 = bf16[16,1,8192]{2,1,0:T(2,128)(2,1)} all-gather(bf16[1,1,8192]{2,1,0:T(2,128)(2,1)S(1)} %get-tuple-element.20), channel_id=5, replica_groups=mesh['rep'=16,'tp'=16] {'tp'}, dimensions={0}, use_global_device_ids=true | all-gather | bytes 278528 | tf_op jit(solution)/shard_map/all_gather | solution.py:100
  233.7 27.0 %all-gather.2 = bf16[16,1,8192]{2,1,0:T(2,128)(2,1)} all-gather(bf16[1,1,8192]{2,1,0:T(2,128)(2,1)S(1)} %get-tuple-element.17), channel_id=4, replica_groups=mesh['rep'=16,'tp'=16] {'tp'}, dimensions={0}, use_global_device_ids=true | all-gather | bytes 278528 | tf_op jit(solution)/shard_map/all_gather | solution.py:100
  260.7 6.1 %add_convert_fusion = bf16[8192,512]{0,1:T(8,128)(2,1)S(1)} fusion(bf16[8192,512]{0,1:T(8,128)(2,1)} %copy.86, bf16[64,512]{1,0:T(8,128)(2,1)S(1)} %reshape.986, bf16[3,8192,64]{1,2,0:T(8,128)(2,1)} %all-gather.9.cloned.1.call-done), kind=kOutput, calls=%fused_computation | convolution fusion | flops 553648128 | bytes 17891328 | tf_op jit(solution)/shard_map/dot_general | solution.py:88
  280.3 6.6 %fusion.14 = bf16[16,576]{1,0:T(8,128)(2,1)S(1)} fusion(bf16[16,1,8192]{2,1,0:T(2,128)(2,1)} %all-gather.2, bf16[8192,32]{0,1:T(8,128)(2,1)} %copy-done.29, bf16[8192,32]{0,1:T(8,128)(2,1)} %copy-done.28, bf16[8192,512]{0,1:T(8,128)(2,1)} %copy-done), kind=kOutput, calls=%fused_computation.30 | convolution fusion | flops 179315712 | bytes 9717760 | tf_op jit(solution)/shard_map/dot_general | solution.py:99
  289.6 7.6 %all-to-all-start.9 = ((bf16[16,1,32]{2,1,0:T(2,128)(2,1)}), bf16[16,1,32]{2,1,0:T(2,128)(2,1)S(1)}, u32[]{:S(2)}, u32[]{:S(2)}) async-start(bf16[16,1,32]{2,1,0:T(2,128)(2,1)} %copy.108), calls=%async_computation.9 | async-start | bytes 16384 | tf_op jit(solution)/shard_map/all_to_all | solution.py:108
  306.6 9.5 %all-to-all-start.1 = ((bf16[16,1,32]{2,1,0:T(2,128)(2,1)}), bf16[16,1,32]{2,1,0:T(2,128)(2,1)S(1)}, u32[]{:S(2)}, u32[]{:S(2)}) async-start(bf16[16,1,32]{2,1,0:T(2,128)(2,1)} %copy.90), calls=%async_computation.1 | async-start | bytes 16384 | tf_op jit(solution)/shard_map/all_to_all | solution.py:108
  316.5 9.0 %all-to-all-done.1 = bf16[16,1,32]{2,1,0:T(2,128)(2,1)S(1)} async-done(((bf16[16,1,32]{2,1,0:T(2,128)(2,1)}), bf16[16,1,32]{2,1,0:T(2,128)(2,1)S(1)}, u32[]{:S(2)}, u32[]{:S(2)}) %all-to-all-start.1) | async-done | bytes 1056 | tf_op jit(solution)/shard_map/all_to_all | solution.py:108
  329.4 9.4 %all-to-all-done.2 = bf16[16,1,32]{2,1,0:T(2,128)(2,1)S(1)} async-done(((bf16[16,1,32]{2,1,0:T(2,128)(2,1)}), bf16[16,1,32]{2,1,0:T(2,128)(2,1)S(1)}, u32[]{:S(2)}, u32[]{:S(2)}) %all-to-all-start.2) | async-done | bytes 1056 | tf_op jit(solution)/shard_map/all_to_all | solution.py:115
  343.2 8.8 %all-to-all-done.5 = bf16[16,1,32]{2,1,0:T(2,128)(2,1)S(1)} async-done(((bf16[16,1,32]{2,1,0:T(2,128)(2,1)}), bf16[16,1,32]{2,1,0:T(2,128)(2,1)S(1)}, u32[]{:S(2)}, u32[]{:S(2)}) %all-to-all-start.5) | async-done | bytes 1056 | tf_op jit(solution)/shard_map/all_to_all | solution.py:108
  356.5 8.8 %all-to-all-done.6 = bf16[16,1,32]{2,1,0:T(2,128)(2,1)S(1)} async-done(((bf16[16,1,32]{2,1,0:T(2,128)(2,1)}), bf16[16,1,32]{2,1,0:T(2,128)(2,1)S(1)}, u32[]{:S(2)}, u32[]{:S(2)}) %all-to-all-start.6) | async-done | bytes 1056 | tf_op jit(solution)/shard_map/all_to_all | solution.py:115
  369.9 8.8 %all-to-all-done.10 = bf16[16,1,32]{2,1,0:T(2,128)(2,1)S(1)} async-done(((bf16[16,1,32]{2,1,0:T(2,128)(2,1)}), bf16[16,1,32]{2,1,0:T(2,128)(2,1)S(1)}, u32[]{:S(2)}, u32[]{:S(2)}) %all-to-all-start.10) | async-done | bytes 1056 | tf_op jit(solution)/shard_map/all_to_all | solution.py:115
  383.6 8.3 %all-to-all-done.14 = bf16[16,1,32]{2,1,0:T(2,128)(2,1)S(1)} async-done(((bf16[16,1,32]{2,1,0:T(2,128)(2,1)}), bf16[16,1,32]{2,1,0:T(2,128)(2,1)S(1)}, u32[]{:S(2)}, u32[]{:S(2)}) %all-to-all-start.14) | async-done | bytes 1056 | tf_op jit(solution)/shard_map/all_to_all | solution.py:115
  411.3 8.9 %all-to-all-done.8 = bf16[16,2,256]{2,1,0:T(2,128)(2,1)S(1)} async-done(((bf16[16,2,256]{2,1,0:T(2,128)(2,1)}), bf16[16,2,256]{2,1,0:T(2,128)(2,1)S(1)}, u32[]{:S(2)}, u32[]{:S(2)}) %all-to-all-start.8) | async-done | bytes 16416 | tf_op jit(solution)/shard_map/all_to_all | solution.py:105
  434.4 8.0 %all-to-all-start = ((bf16[16,2,256]{2,1,0:T(2,128)(2,1)}), bf16[16,2,256]{2,1,0:T(2,128)(2,1)}, u32[]{:S(2)}, u32[]{:S(2)}) async-start(bf16[16,2,256]{2,1,0:T(2,128)(2,1)} %reshape.1030), calls=%async_computation | async-start | bytes 32768 | tf_op jit(solution)/shard_map/all_to_all | solution.py:105
  462.0 6.6 %all-to-all-start.3 = ((bf16[16,2,256]{2,1,0:T(2,128)(2,1)}), bf16[16,2,256]{2,1,0:T(2,128)(2,1)S(1)}, u32[]{:S(2)}, u32[]{:S(2)}) async-start(bf16[16,2,256]{2,1,0:T(2,128)(2,1)} %reshape.1042), calls=%async_computation.3 | async-start | bytes 32768 | tf_op jit(solution)/shard_map/all_to_all | solution.py:135
  484.5 8.1 %all-to-all-done.7 = bf16[16,2,256]{2,1,0:T(2,128)(2,1)S(1)} async-done(((bf16[16,2,256]{2,1,0:T(2,128)(2,1)}), bf16[16,2,256]{2,1,0:T(2,128)(2,1)S(1)}, u32[]{:S(2)}, u32[]{:S(2)}) %all-to-all-start.7) | async-done | bytes 16416 | tf_op jit(solution)/shard_map/all_to_all | solution.py:135
  497.8 8.2 %all-to-all-done.11 = bf16[16,2,256]{2,1,0:T(2,128)(2,1)S(1)} async-done(((bf16[16,2,256]{2,1,0:T(2,128)(2,1)}), bf16[16,2,256]{2,1,0:T(2,128)(2,1)S(1)}, u32[]{:S(2)}, u32[]{:S(2)}) %all-to-all-start.11) | async-done | bytes 16416 | tf_op jit(solution)/shard_map/all_to_all | solution.py:135
  511.0 8.5 %all-to-all-done.15 = bf16[16,2,256]{2,1,0:T(2,128)(2,1)S(1)} async-done(((bf16[16,2,256]{2,1,0:T(2,128)(2,1)}), bf16[16,2,256]{2,1,0:T(2,128)(2,1)S(1)}, u32[]{:S(2)}, u32[]{:S(2)}) %all-to-all-start.15) | async-done | bytes 16416 | tf_op jit(solution)/shard_map/all_to_all | solution.py:135
  (211 shorter events, 131.6 us)
Async XLA Ops:
  7.2 253.5 %all-gather.9.cloned.1.call-start = ((), (), s32[]{:S(2)}) async-start(), calls=%async_computation.16 | async-start | bytes 3342336 | tf_op jit(solution)/shard_map/all_gather | solution.py:81
  7.9 55.2 %copy-start.24 = (bf16[4,32]{1,0:T(4,128)(2,1)S(1)}, bf16[4,32]{1,0:T(4,128)(2,1)}, u32[]{:S(2)}) copy-start(bf16[4,32]{1,0:T(4,128)(2,1)} %param.17) | copy-start | bytes 772
  7.9 86.3 %copy-start.25 = (bf16[4,32]{1,0:T(4,128)(2,1)S(1)}, bf16[4,32]{1,0:T(4,128)(2,1)}, u32[]{:S(2)}) copy-start(bf16[4,32]{1,0:T(4,128)(2,1)} %param.18) | copy-start | bytes 772
  7.9 119.3 %copy-start.7 = (bf16[4,1,8192]{2,0,1:T(4,128)(2,1)S(1)}, bf16[4,1,8192]{2,0,1:T(4,128)(2,1)}, u32[]{:S(2)}) copy-start(bf16[4,1,8192]{2,0,1:T(4,128)(2,1)} %param.11) | copy-start | bytes 196612
  127.0 269.0 %copy-start.18 = (f32[64]{0:T(128)}, f32[64]{0:T(128)S(1)}, u32[]{:S(2)}) copy-start(f32[64]{0:T(128)S(1)} %get-tuple-element.69) | copy-start | bytes 772
  127.0 269.0 %copy-start.19 = (f32[64]{0:T(128)}, f32[64]{0:T(128)S(1)}, u32[]{:S(2)}) copy-start(f32[64]{0:T(128)S(1)} %get-tuple-element.70) | copy-start | bytes 772
  127.2 269.6 %copy-start.16 = (f32[64]{0:T(128)}, f32[64]{0:T(128)S(1)}, u32[]{:S(2)}) copy-start(f32[64]{0:T(128)S(1)} %get-tuple-element.63) | copy-start | bytes 772
  127.2 269.6 %copy-start.17 = (f32[64]{0:T(128)}, f32[64]{0:T(128)S(1)}, u32[]{:S(2)}) copy-start(f32[64]{0:T(128)S(1)} %get-tuple-element.64) | copy-start | bytes 772
  276.1 13.5 %all-to-all-start.13 = ((bf16[16,1,32]{2,1,0:T(2,128)(2,1)}), bf16[16,1,32]{2,1,0:T(2,128)(2,1)S(1)}, u32[]{:S(2)}, u32[]{:S(2)}) async-start(bf16[16,1,32]{2,1,0:T(2,128)(2,1)} %copy.119), calls=%async_computation.13 | async-start | bytes 16384 | tf_op jit(solution)/shard_map/all_to_all | solution.py:108
  289.6 17.0 %all-to-all-start.9 = ((bf16[16,1,32]{2,1,0:T(2,128)(2,1)}), bf16[16,1,32]{2,1,0:T(2,128)(2,1)S(1)}, u32[]{:S(2)}, u32[]{:S(2)}) async-start(bf16[16,1,32]{2,1,0:T(2,128)(2,1)} %copy.108), calls=%async_computation.9 | async-start | bytes 16384 | tf_op jit(solution)/shard_map/all_to_all | solution.py:108
  306.6 18.9 %all-to-all-start.1 = ((bf16[16,1,32]{2,1,0:T(2,128)(2,1)}), bf16[16,1,32]{2,1,0:T(2,128)(2,1)S(1)}, u32[]{:S(2)}, u32[]{:S(2)}) async-start(bf16[16,1,32]{2,1,0:T(2,128)(2,1)} %copy.90), calls=%async_computation.1 | async-start | bytes 16384 | tf_op jit(solution)/shard_map/all_to_all | solution.py:108
  325.5 13.2 %all-to-all-start.2 = ((bf16[16,1,32]{2,1,0:T(2,128)(2,1)}), bf16[16,1,32]{2,1,0:T(2,128)(2,1)S(1)}, u32[]{:S(2)}, u32[]{:S(2)}) async-start(bf16[16,1,32]{2,1,0:T(2,128)(2,1)} %copy.92), calls=%async_computation.2 | async-start | bytes 16384 | tf_op jit(solution)/shard_map/all_to_all | solution.py:115
  338.8 13.2 %all-to-all-start.5 = ((bf16[16,1,32]{2,1,0:T(2,128)(2,1)}), bf16[16,1,32]{2,1,0:T(2,128)(2,1)S(1)}, u32[]{:S(2)}, u32[]{:S(2)}) async-start(bf16[16,1,32]{2,1,0:T(2,128)(2,1)} %copy.98), calls=%async_computation.5 | async-start | bytes 16384 | tf_op jit(solution)/shard_map/all_to_all | solution.py:108
  352.0 13.3 %all-to-all-start.6 = ((bf16[16,1,32]{2,1,0:T(2,128)(2,1)}), bf16[16,1,32]{2,1,0:T(2,128)(2,1)S(1)}, u32[]{:S(2)}, u32[]{:S(2)}) async-start(bf16[16,1,32]{2,1,0:T(2,128)(2,1)} %copy.101), calls=%async_computation.6 | async-start | bytes 16384 | tf_op jit(solution)/shard_map/all_to_all | solution.py:115
  365.3 13.4 %all-to-all-start.10 = ((bf16[16,1,32]{2,1,0:T(2,128)(2,1)}), bf16[16,1,32]{2,1,0:T(2,128)(2,1)S(1)}, u32[]{:S(2)}, u32[]{:S(2)}) async-start(bf16[16,1,32]{2,1,0:T(2,128)(2,1)} %copy.111), calls=%async_computation.10 | async-start | bytes 16384 | tf_op jit(solution)/shard_map/all_to_all | solution.py:115
  378.7 13.2 %all-to-all-start.14 = ((bf16[16,1,32]{2,1,0:T(2,128)(2,1)}), bf16[16,1,32]{2,1,0:T(2,128)(2,1)S(1)}, u32[]{:S(2)}, u32[]{:S(2)}) async-start(bf16[16,1,32]{2,1,0:T(2,128)(2,1)} %copy.122), calls=%async_computation.14 | async-start | bytes 16384 | tf_op jit(solution)/shard_map/all_to_all | solution.py:115
  391.9 13.7 %all-to-all-start.12 = ((bf16[16,2,256]{2,1,0:T(2,128)(2,1)}), bf16[16,2,256]{2,1,0:T(2,128)(2,1)S(1)}, u32[]{:S(2)}, u32[]{:S(2)}) async-start(bf16[16,2,256]{2,1,0:T(2,128)(2,1)} %reshape.1028), calls=%async_computation.12 | async-start | bytes 32768 | tf_op jit(solution)/shard_map/all_to_all | solution.py:105
  405.6 14.7 %all-to-all-start.8 = ((bf16[16,2,256]{2,1,0:T(2,128)(2,1)}), bf16[16,2,256]{2,1,0:T(2,128)(2,1)S(1)}, u32[]{:S(2)}, u32[]{:S(2)}) async-start(bf16[16,2,256]{2,1,0:T(2,128)(2,1)} %reshape.1034), calls=%async_computation.8 | async-start | bytes 32768 | tf_op jit(solution)/shard_map/all_to_all | solution.py:105
  420.3 14.1 %all-to-all-start.4 = ((bf16[16,2,256]{2,1,0:T(2,128)(2,1)}), bf16[16,2,256]{2,1,0:T(2,128)(2,1)}, u32[]{:S(2)}, u32[]{:S(2)}) async-start(bf16[16,2,256]{2,1,0:T(2,128)(2,1)} %reshape.1032), calls=%async_computation.4 | async-start | bytes 32768 | tf_op jit(solution)/shard_map/all_to_all | solution.py:105
  434.4 17.8 %all-to-all-start = ((bf16[16,2,256]{2,1,0:T(2,128)(2,1)}), bf16[16,2,256]{2,1,0:T(2,128)(2,1)}, u32[]{:S(2)}, u32[]{:S(2)}) async-start(bf16[16,2,256]{2,1,0:T(2,128)(2,1)} %reshape.1030), calls=%async_computation | async-start | bytes 32768 | tf_op jit(solution)/shard_map/all_to_all | solution.py:105
  462.0 16.3 %all-to-all-start.3 = ((bf16[16,2,256]{2,1,0:T(2,128)(2,1)}), bf16[16,2,256]{2,1,0:T(2,128)(2,1)S(1)}, u32[]{:S(2)}, u32[]{:S(2)}) async-start(bf16[16,2,256]{2,1,0:T(2,128)(2,1)} %reshape.1042), calls=%async_computation.3 | async-start | bytes 32768 | tf_op jit(solution)/shard_map/all_to_all | solution.py:135
  478.3 14.2 %all-to-all-start.7 = ((bf16[16,2,256]{2,1,0:T(2,128)(2,1)}), bf16[16,2,256]{2,1,0:T(2,128)(2,1)S(1)}, u32[]{:S(2)}, u32[]{:S(2)}) async-start(bf16[16,2,256]{2,1,0:T(2,128)(2,1)} %reshape.1040), calls=%async_computation.7 | async-start | bytes 32768 | tf_op jit(solution)/shard_map/all_to_all | solution.py:135
  492.6 13.4 %all-to-all-start.11 = ((bf16[16,2,256]{2,1,0:T(2,128)(2,1)}), bf16[16,2,256]{2,1,0:T(2,128)(2,1)S(1)}, u32[]{:S(2)}, u32[]{:S(2)}) async-start(bf16[16,2,256]{2,1,0:T(2,128)(2,1)} %reshape.1038), calls=%async_computation.11 | async-start | bytes 32768 | tf_op jit(solution)/shard_map/all_to_all | solution.py:135
  506.0 13.4 %all-to-all-start.15 = ((bf16[16,2,256]{2,1,0:T(2,128)(2,1)}), bf16[16,2,256]{2,1,0:T(2,128)(2,1)S(1)}, u32[]{:S(2)}, u32[]{:S(2)}) async-start(bf16[16,2,256]{2,1,0:T(2,128)(2,1)} %reshape.1036), calls=%async_computation.15 | async-start | bytes 32768 | tf_op jit(solution)/shard_map/all_to_all | solution.py:135
  (23 other events, 489.2 us)
Sparse Core Ops, SparseCore 0:
  9.8 87.9 all-gather.8
where the time goes:
time: 529 us; the launch traced here: 527 us
  blocking collectives  237 us (45%)
  waiting for transfers between devices  104 us (20%)
  starting transfers between devices  80.1 us (15%)
  matrix products  37.8 us (7%)
  local copies, waits for them, and re-layouts  33.2 us (6%)
  other arithmetic  19.2 us (4%)
  between operations  15.4 us (3%)
    all_gather x4, blocking collectives, shards(): lax.all_gather(hidden[step_index], 'tp', axis=0, tiled=True)  133 us
    all_gather x1, blocking collectives, shards(): lax.all_gather(b_query, 'rep', axis=0, tiled=True)  40.2 us
    all_to_all x4, waiting for transfers between devices, shards(): lax.all_to_all(projected[:, query_cols + key_cols:], 'tp', split_axis=0,...  35.2 us
    all_gather x1, blocking collectives, shards(): lax.all_gather(b_value, 'rep', axis=0, tiled=True)  32.6 us
    all_gather x1, blocking collectives, shards(): lax.all_gather(b_key, 'rep', axis=0, tiled=True)  31.1 us
    all_to_all x4, waiting for transfers between devices, shards(): lax.all_to_all(attended, 'tp', split_axis=1, concat_axis=0, tiled=True)  29.9 us
    all_to_all x4, starting transfers between devices, shards(): lax.all_to_all(projected[:, query_cols:query_cols + key_cols], 'tp', spli...  25.1 us
    all_to_all x4, starting transfers between devices, shards(): lax.all_to_all(projected[:, :query_cols], 'tp', split_axis=0, concat_axis...  21.2 us
  transfers between devices with their start and end apart: 17, of which 16 were waited for; matrix products, arithmetic and copies ran while one was open for 12% of the time, Pallas kernels for 0%

commit v1 on v0

v1 whole, which is shorter than its diff:
```python
import functools
import math

import jax
import jax.numpy as jnp
from jax import lax
from jax.experimental import pallas as pl
from jax.experimental.pallas import tpu as pltpu
from jax.sharding import PartitionSpec as P

HEAD_DIM = 128
STEPS = 4
THETA = 500000.0
SCALE = 0.5
MESH = pl.DeviceIdType.MESH
F32 = jnp.float32
BF16 = jnp.bfloat16

SLOTS = 1536
KEYS = SLOTS + 128
WIDTH = 8192
HALF = WIDTH // 2


def offset(index):
    return (index * (index + 1) // 2) % 4


def body(
    lengths_ref, hidden_ref, wq_ref, wk_ref, wv_ref, a_ref, bq_ref, bk_ref, bv_ref,
    keys_ref, values_ref, cos_ref, sin_ref,
    out_ref, new_keys_ref, new_values_ref,
    wq, wkv, a_buf, h_buf, k_buf, v_buf,
    b_f32, b_send, b_recv, b_query, b_kv,
    h_f32, h_send, h_recv, g_f32,
    acc_q, acc_kv, q_f32, q_send, q_recv, o_send, o_recv, o_f32,
    local_sem, b_ssem, b_rsem, hx_ssem, hx_rsem, x_ssem, x_rsem, hs_ssem, hs_rsem,
    f_ssem, s_ssem, fwd_ssem, a_rsem, sib_ssem, sib_rsem,
    q_ssem, q_rsem, o_ssem, o_rsem,
):
    r = lax.axis_index("rep")
    t = lax.axis_index("tp")
    y, zl = r // 4, r % 4
    zh, x, c = t // 8, (t // 2) % 4, t % 2
    z = zh * 4 + zl
    other = 1 - c

    def tp_of(high, at_x, core):
        return (high * 4 + at_x) * 2 + core

    def z_step(delta):
        to = (z + 8 + delta) % 8
        return y * 4 + to % 4, tp_of(to // 4, x, c)

    def y_step(delta):
        return ((y + 4 + delta) % 4) * 4 + zl, t

    def pick(first):
        devices = []
        for delta in (1, -1):
            zr, zt = z_step(delta)
            yr, yt = y_step(delta)
            is_y = c if first else other
            devices.append((is_y * yr + (1 - is_y) * zr, is_y * yt + (1 - is_y) * zt))
        return devices

    f_plus, f_minus = pick(True)
    s_plus, s_minus = pick(False)
    sibling = (r, tp_of(zh, x, other))

    def origin(core, slot):
        df, ds = offset(slot // 4), offset(slot % 4)
        at_y = (y + core * df + (1 - core) * ds) % 4
        at_z = (zl + (1 - core) * df + core * ds) % 4
        return at_y * 4 + at_z

    def remote(src, dst, ssem, rsem, device):
        return pltpu.make_async_remote_copy(
            src_ref=src, dst_ref=dst, send_sem=ssem, recv_sem=rsem,
            device_id=device, device_id_type=MESH,
        )

    loads = [
        pltpu.make_async_copy(a_ref.at[:, pl.ds(0, 256)], a_buf.at[r, 0], local_sem.at[0]),
        pltpu.make_async_copy(a_ref.at[:, pl.ds(256, 256)], a_buf.at[r, 1], local_sem.at[1]),
        pltpu.make_async_copy(wq_ref, wq, local_sem.at[2]),
        pltpu.make_async_copy(wk_ref, wkv.at[pl.ds(0, 32)], local_sem.at[3]),
        pltpu.make_async_copy(wv_ref, wkv.at[pl.ds(32, 32)], local_sem.at[4]),
        pltpu.make_async_copy(keys_ref, k_buf.at[pl.ds(0, SLOTS)], local_sem.at[5]),
        pltpu.make_async_copy(values_ref, v_buf.at[pl.ds(0, SLOTS)], local_sem.at[6]),
    ]
    for load in loads:
        load.start()

    barrier = pltpu.get_barrier_semaphore()

    def greet(step, _):
        pl.semaphore_signal(barrier, inc=1, device_id=(r, (t + step) % 16), device_id_type=MESH)
        pl.semaphore_signal(barrier, inc=1, device_id=((r + step) % 16, t), device_id_type=MESH)
        return 0

    lax.fori_loop(1, 16, greet, 0)
    for delta in (1, -1):
        pl.semaphore_signal(barrier, inc=1, device_id=z_step(delta), device_id_type=MESH)

    b_f32[...] = jnp.zeros_like(b_f32)
    up = bq_ref[...].astype(F32)
    up_key = bk_ref[...].astype(F32)
    up_value = bv_ref[...].astype(F32)
    for k in range(4):
        for h in range(4):
            b_f32[8 * k + h : 8 * k + h + 1, :] = up[k : k + 1, 128 * h : 128 * h + 128]
        b_f32[8 * k + 4 : 8 * k + 5, 0:32] = up_key[k : k + 1, :]
        b_f32[8 * k + 5 : 8 * k + 6, 0:32] = up_value[k : k + 1, :]
    b_send[...] = b_f32[0:32, :].astype(BF16)
    own = hidden_ref[...].astype(F32)
    for half in range(2):
        for block in range(4):
            start = half * HALF + block * 1024
            h_f32[half, 4 * block : 4 * block + 4, :] = own[:, start : start + 1024]
    h_send[...] = h_f32[...].astype(BF16)
    k_buf[SLOTS:, :] = jnp.zeros((128, 512), BF16)
    v_buf[SLOTS:, :] = jnp.zeros((128, 512), BF16)
    loads[0].wait()
    loads[1].wait()
    pl.semaphore_wait(barrier, 32)

    def b_copy(step):
        return remote(b_send, b_recv.at[r], b_ssem.at[step], b_rsem.at[step], ((r + step) % 16, t))

    def start_b(step, _):
        b_copy(step).start()
        return 0

    lax.fori_loop(1, 16, start_b, 0)
    b_recv[r] = b_send[...]

    me4 = zh * 2 + c
    hx = []
    for at, (to_high, to_core) in enumerate(((zh, other), (1 - zh, c), (1 - zh, other))):
        hx.append(remote(
            h_send.at[to_core], h_recv.at[me4], hx_ssem.at[at], hx_rsem.at[at],
            (r, tp_of(to_high, x, to_core)),
        ))
    for copy in reversed(hx):
        copy.start()
    h_recv[me4] = h_send[c]

    def f_copy(kind):
        if kind == 0:
            mine = a_buf.at[r, c]
            return remote(mine, mine, f_ssem.at[0], a_rsem.at[8, 0], f_plus)
        if kind == 1:
            mine = a_buf.at[r, c]
            return remote(mine, mine, f_ssem.at[1], a_rsem.at[4, 0], f_minus)
        if kind == 2:
            part = a_buf.at[origin(c, 8), c, pl.ds(0, 96)]
            return remote(part, part, f_ssem.at[2], a_rsem.at[12, 0], f_plus)
        part = a_buf.at[origin(c, 4), c, pl.ds(96, 96)]
        return remote(part, part, f_ssem.at[3], a_rsem.at[12, 1], f_minus)

    def s_copy(index, way):
        chunk = a_buf.at[origin(c, index * 4), c]
        return remote(
            chunk, chunk, s_ssem.at[index, way], a_rsem.at[index * 4 + 2 - way, 0],
            s_plus if way == 0 else s_minus,
        )

    def fwd_copy(index, way):
        part = a_buf.at[origin(c, index * 4 + 2 - way), c, pl.ds(96 * way, 96)]
        return remote(
            part, part, fwd_ssem.at[index, way], a_rsem.at[index * 4 + 3, way],
            s_plus if way == 0 else s_minus,
        )

    def sib_copy(slot):
        chunk = a_buf.at[origin(c, slot), c]
        return remote(chunk, chunk, sib_ssem.at[slot], sib_rsem.at[slot], sibling)

    def sib_in(slot):
        chunk = a_buf.at[origin(other, slot), other]
        return remote(chunk, chunk, sib_ssem.at[slot], sib_rsem.at[slot], sibling)

    def a_in(slot, part=None):
        chunk = a_buf.at[origin(c, slot), c]
        if part is not None:
            chunk = chunk.at[pl.ds(96 * part, 96)]
        return remote(
            chunk, chunk, sib_ssem.at[slot], a_rsem.at[slot, 0 if part is None else part], sibling
        )

    f_copy(0).start()
    f_copy(1).start()
    s_copy(0, 0).start()
    s_copy(0, 1).start()

    def half_of(at_x, core, start=0, size=HALF):
        return h_buf.at[at_x, :, pl.ds(pl.multiple_of(core * HALF + start, 128), size)]

    x_plus = (r, tp_of(zh, (x + 1) % 4, c))
    x_minus = (r, tp_of(zh, (x + 3) % 4, c))

    def x_copy(kind):
        if kind < 2:
            block = half_of(x, c)
            return remote(block, block, x_ssem.at[kind], x_rsem.at[kind], (x_plus, x_minus)[kind])
        source = (x + 3) % 4 if kind == 2 else (x + 1) % 4
        block = half_of(source, c, (kind - 2) * 2048, 2048)
        return remote(block, block, x_ssem.at[kind], x_rsem.at[kind], (x_plus, x_minus)[kind - 2])

    def hs_copy(step):
        block = half_of((x + step) % 4, c)
        return remote(block, block, hs_ssem.at[step], hs_rsem.at[step], sibling)

    def hs_in(step):
        block = half_of((x + step) % 4, other)
        return remote(block, block, hs_ssem.at[step], hs_rsem.at[step], sibling)

    def x_in(kind):
        if kind < 2:
            block = half_of((x + 3) % 4 if kind == 0 else (x + 1) % 4, c)
        else:
            block = half_of((x + 2) % 4, c, (kind - 2) * 2048, 2048)
        return remote(block, block, x_ssem.at[kind], x_rsem.at[kind], sibling)

    for copy in hx:
        copy.wait_recv()
    for k in range(4):
        got = h_recv[k].astype(F32)
        for block in range(4):
            g_f32[4 * k : 4 * k + 4, 1024 * block : 1024 * block + 1024] = got[
                4 * block : 4 * block + 4, :
            ]
    h_buf[x, :, pl.ds(pl.multiple_of(c * HALF, 128), HALF)] = g_f32[...].astype(BF16)
    x_copy(0).start()
    x_copy(1).start()
    hs_copy(0).start()

    def wait_b(step, _):
        b_copy(step).wait_recv()
        return 0

    lax.fori_loop(1, 16, wait_b, 0)
    b_f32[...] = b_recv[...].reshape(512, 128).astype(F32)
    for h in range(4):
        b_query[:, 128 * h : 128 * h + 128] = (SCALE * b_f32[pl.ds(h, 64, stride=8), :]).astype(BF16)
    bk_all = SCALE * b_f32[pl.ds(4, 64, stride=8), :]
    bv_all = SCALE * b_f32[pl.ds(5, 64, stride=8), :]
    b_kv[:, 0:64] = jnp.transpose(bk_all)[0:64, :].astype(BF16)
    b_kv[:, 64:128] = jnp.transpose(pltpu.roll(bv_all, 32, 1))[0:64, :].astype(BF16)

    acc_q[...] = jnp.zeros_like(acc_q)
    acc_kv[...] = jnp.zeros_like(acc_kv)
    for load in loads[2:5]:
        load.wait()

    def merge(at, half):
        start = pl.multiple_of(at * 512 + half * 256, 256)
        down = a_buf[at, half]
        low = lax.dot_general(
            down[0:64], b_query[...], (((0,), (0,)), ((), ())), preferred_element_type=F32
        )
        rows = pl.ds(start, 256)
        wq[rows, :] = (wq[rows, :].astype(F32) + low).astype(BF16)
        low_kv = jnp.dot(b_kv[...], down[64:192], preferred_element_type=F32)
        wkv[:, rows] = (wkv[:, rows].astype(F32) + low_kv).astype(BF16)

    def project(slot):
        start = pl.multiple_of(origin(c, slot) * 512, 512)
        states = h_buf[:, :, pl.ds(start, 512)].reshape(64, 512)
        acc_q[...] += jnp.dot(states, wq[pl.ds(start, 512), :], preferred_element_type=F32)
        acc_kv[...] += lax.dot_general(
            states, wkv[:, pl.ds(start, 512)], (((1,), (1,)), ((), ())), preferred_element_type=F32
        )

    def turn(slot, _):
        index, way = slot // 4, slot % 4

        @pl.when(slot == 1)
        def _():
            a_in(4).wait_recv()
            s_copy(1, 0).start()
            s_copy(1, 1).start()
            f_copy(3).start()
            sib_copy(4).start()

        @pl.when(slot == 2)
        def _():
            a_in(8).wait_recv()
            s_copy(2, 0).start()
            s_copy(2, 1).start()
            f_copy(2).start()
            sib_copy(8).start()

        @pl.when(slot == 3)
        def _():
            a_in(12, 0).wait_recv()
            a_in(12, 1).wait_recv()
            s_copy(3, 0).start()
            s_copy(3, 1).start()
            sib_copy(12).start()

        @pl.when(way == 1)
        def _():
            a_in(slot).wait_recv()
            fwd_copy(index, 1).start()
            sib_copy(slot).start()

        @pl.when(way == 2)
        def _():
            a_in(slot).wait_recv()
            fwd_copy(index, 0).start()
            sib_copy(slot).start()

        @pl.when(way == 3)
        def _():
            a_in(slot, 0).wait_recv()
            a_in(slot, 1).wait_recv()
            sib_copy(slot).start()

        @pl.when(slot == 4)
        def _():
            x_in(0).wait_recv()
            x_in(1).wait_recv()
            x_copy(2).start()
            x_copy(3).start()
            hs_copy(3).start()
            hs_copy(1).start()

        @pl.when(slot == 6)
        def _():
            x_in(2).wait_recv()
            x_in(3).wait_recv()
            hs_copy(2).start()

        @pl.when(slot == 8)
        def _():
            for step in range(4):
                hs_in(step).wait_recv()

        merge(origin(c, slot), c)

        @pl.when(slot > 0)
        def _():
            sib_in(slot).wait_recv()

        merge(origin(other, slot), other)

        return 0

    lax.fori_loop(0, 16, turn, 0)

    def project_turn(slot, _):
        project(slot)
        return 0

    lax.fori_loop(0, 16, project_turn, 0)

    acc = acc_q[...]
    kv = jnp.concatenate([acc_kv[...], jnp.zeros((64, 64), F32)], 1)
    lane = lax.broadcasted_iota(jnp.int32, (64, 128), 1)
    mine = lane // 32 == t % 4
    own_key = jnp.where(mine, pltpu.roll(kv, (t % 4) * 32, 1), 0.0)
    own_value = jnp.where(mine, pltpu.roll(kv, (t % 4) * 32 + 96, 1), 0.0)
    for to in range(16):
        base = ((to // 2) % 4) * 16 + ((to // 8) * 2 + to % 2) * 4
        for h in range(4):
            q_f32[to, 4 * h : 4 * h + 4, :] = acc[base : base + 4, 128 * h : 128 * h + 128]
        q_f32[to, 16:20, :] = own_key[base : base + 4]
        q_f32[to, 20:24, :] = own_value[base : base + 4]
        q_f32[to, 24:32, :] = jnp.zeros((8, 128), F32)
    q_send[...] = q_f32[...].astype(BF16)

    def q_copy(step):
        to = (t + step) % 16
        return remote(q_send.at[to], q_recv.at[t], q_ssem.at[step], q_rsem.at[step], (r, to))

    def start_q(step, _):
        q_copy(step).start()
        return 0

    lax.fori_loop(1, 16, start_q, 0)
    q_recv[t] = q_send[t]
    loads[5].wait()
    loads[6].wait()

    def wait_q(step, _):
        q_copy(step).wait_recv()
        return 0

    lax.fori_loop(1, 16, wait_q, 0)

    cosine, sine = cos_ref[...], sin_ref[...]
    length = lengths_ref[0]
    column = lax.broadcasted_iota(jnp.int32, (64, KEYS), 1)
    step_of = lax.broadcasted_iota(jnp.int32, (64, KEYS), 0) % 4
    valid = (column < length) | ((column >= SLOTS) & (column - SLOTS <= step_of))
    scaling = 1.0 / math.sqrt(HEAD_DIM)

    def rotated(values, cos_rows, sin_rows):
        return values * cos_rows + pltpu.roll(values, 64, values.ndim - 1) * sin_rows

    for g in range(4):
        cols = slice(128 * g, 128 * g + 128)
        fresh = q_recv[4 * g, 16:32, :].astype(F32)
        for u in range(1, 4):
            fresh += q_recv[4 * g + u, 16:32, :].astype(F32)
        fresh_key = rotated(fresh, cosine, sine)[0:4].astype(BF16)
        fresh_value = fresh[4:8].astype(BF16)
        new_keys_ref[:, cols] = fresh_key
        new_values_ref[:, cols] = fresh_value
        pad = jnp.zeros((12, 128), BF16)
        k_buf[SLOTS : SLOTS + 16, cols] = jnp.concatenate([fresh_key, pad], 0)
        v_buf[SLOTS : SLOTS + 16, cols] = jnp.concatenate([fresh_value, pad], 0)
        query = q_recv[4 * g : 4 * g + 4, 0:16, :].astype(F32).reshape(64, 128)
        tables = (jnp.concatenate([cosine] * 4, 0), jnp.concatenate([sine] * 4, 0))
        query = rotated(query, *tables).astype(BF16)
        scores = scaling * lax.dot_general(
            query, k_buf[:, cols], (((1,), (1,)), ((), ())), preferred_element_type=F32
        )
        scores = jnp.where(valid, scores, -1e30)
        highest = jnp.max(scores, -1, keepdims=True)
        weights = jnp.where(valid, jnp.exp(scores - highest), 0.0)
        total = jnp.sum(weights, -1, keepdims=True)
        probs = (weights * (1.0 / total)).astype(BF16)
        blended = jnp.dot(probs, v_buf[:, cols], preferred_element_type=F32).astype(BF16)
        o_send[4 * g : 4 * g + 4] = blended.reshape(4, 16, 128)

    def o_copy(step):
        to = (t + step) % 16
        return remote(o_send.at[to], o_recv.at[t], o_ssem.at[step], o_rsem.at[step], (r, to))

    def start_o(step, _):
        o_copy(step).start()
        return 0

    lax.fori_loop(1, 16, start_o, 0)
    o_recv[t] = o_send[t]

    def wait_o(step, _):
        o_copy(step).wait_recv()
        return 0

    lax.fori_loop(1, 16, wait_o, 0)
    o_f32[...] = o_recv[...].reshape(256, 128).astype(F32)
    for s in range(STEPS):
        for h in range(4):
            out_ref[s, :, 128 * h : 128 * h + 128] = o_f32[
                pl.ds(4 * h + s, 16, stride=16), :
            ].astype(BF16)

    def wait_sends(step, _):
        b_copy(step).wait_send()
        q_copy(step).wait_send()
        o_copy(step).wait_send()
        sib_copy(step).wait_send()
        return 0

    lax.fori_loop(1, 16, wait_sends, 0)
    for copy in hx:
        copy.wait_send()
    for k in range(4):
        f_copy(k).wait_send()
        x_copy(k).wait_send()
        hs_copy(k).wait_send()
        for way in range(2):
            s_copy(k, way).wait_send()
            fwd_copy(k, way).wait_send()


def shards(
    hidden, w_query, w_key, w_value, a_factors, b_query, b_key, b_value,
    key_cache, value_cache, lengths,
):
    half_dim = HEAD_DIM // 2
    frequency = THETA ** (-(jnp.arange(half_dim, dtype=F32) * 2.0 / HEAD_DIM))
    positions = lengths[0] + jnp.arange(16, dtype=jnp.int32) % STEPS
    angles = positions.astype(F32)[:, None] * frequency
    cosine, sine = jnp.cos(angles), jnp.sin(angles)
    cosine = jnp.concatenate([cosine, cosine], 1)
    sine = jnp.concatenate([-sine, sine], 1)

    anywhere = pl.BlockSpec(memory_space=pl.ANY)
    vmem = pl.BlockSpec(memory_space=pltpu.VMEM)
    dma = pltpu.SemaphoreType.DMA
    attended, new_keys, new_values = pl.pallas_call(
        body,
        out_shape=(
            jax.ShapeDtypeStruct((4, 16, 512), BF16),
            jax.ShapeDtypeStruct((4, 512), BF16),
            jax.ShapeDtypeStruct((4, 512), BF16),
        ),
        in_specs=[
            pl.BlockSpec(memory_space=pltpu.SMEM), vmem, anywhere, anywhere, anywhere, anywhere,
            vmem, vmem, vmem, anywhere, anywhere, vmem, vmem,
        ],
        out_specs=(vmem, vmem, vmem),
        scratch_shapes=[
            pltpu.VMEM((WIDTH, 512), BF16),
            pltpu.VMEM((64, WIDTH), BF16),
            pltpu.VMEM((16, 2, 192, 256), BF16),
            pltpu.VMEM((4, 16, WIDTH), BF16),
            pltpu.VMEM((KEYS, 512), BF16),
            pltpu.VMEM((KEYS, 512), BF16),
            pltpu.VMEM((512, 128), F32),
            pltpu.VMEM((32, 128), BF16),
            pltpu.VMEM((16, 32, 128), BF16),
            pltpu.VMEM((64, 512), BF16),
            pltpu.VMEM((64, 128), BF16),
            pltpu.VMEM((2, 16, 1024), F32),
            pltpu.VMEM((2, 16, 1024), BF16),
            pltpu.VMEM((4, 16, 1024), BF16),
            pltpu.VMEM((16, HALF), F32),
            pltpu.VMEM((64, 512), F32),
            pltpu.VMEM((64, 64), F32),
            pltpu.VMEM((16, 32, 128), F32),
            pltpu.VMEM((16, 32, 128), BF16),
            pltpu.VMEM((16, 32, 128), BF16),
            pltpu.VMEM((16, 16, 128), BF16),
            pltpu.VMEM((16, 16, 128), BF16),
            pltpu.VMEM((256, 128), F32),
            dma((7,)), dma((16,)), dma((16,)), dma((3,)), dma((3,)),
            dma((4,)), dma((4,)), dma((4,)), dma((4,)),
            dma((4,)), dma((4, 2)), dma((4, 2)), dma((16, 2)), dma((16,)), dma((16,)),
            dma((16,)), dma((16,)), dma((16,)), dma((16,)),
        ],
        compiler_params=pltpu.CompilerParams(
            collective_id=0, has_side_effects=True, vmem_limit_bytes=48 * 1024 * 1024
        ),
    )(
        lengths, hidden[:, 0], w_query, w_key.T, w_value.T,
        jnp.swapaxes(a_factors, 1, 2).reshape(192, 512), b_query, b_key, b_value,
        key_cache[0], value_cache[0], cosine, sine,
    )
    return attended, new_keys[:, None], new_values[:, None]


def solution(mesh):
    placed = (
        P(None, ("rep", "tp"), None),
        P(None, "tp"),
        P(None, "tp"),
        P(None, "tp"),
        P(None, "rep", None),
        P("rep", "tp"),
        P("rep", "tp"),
        P("rep", "tp"),
        P(("rep", "tp"), None, None),
        P(("rep", "tp"), None, None),
        P(("rep", "tp")),
    )
    return jax.shard_map(
        shards,
        mesh=mesh,
        in_specs=placed,
        out_specs=(
            P(None, "rep", "tp"),
            P(None, ("rep", "tp"), None),
            P(None, ("rep", "tp"), None),
        ),
        check_vma=False,
    )
```

time: 529 us -> 84.9 us (0.16)
  blocking collectives: 237 us -> 0 us
  waiting for transfers between devices: 104 us -> 0 us
  starting transfers between devices: 80.1 us -> 0 us
  Pallas kernels: 0 us -> 72.5 us
  matrix products: 37.8 us -> 0 us
  local copies, waits for them, and re-layouts: 33.2 us -> 10.5 us
  other arithmetic: 19.2 us -> 0.21 us
  between operations: 15.4 us -> 1.31 us
    all_gather x7 -> x0, blocking collectives: 237 us -> none  [the longest x4 133 us: shards(): lax.all_gather(hidden[step_index], 'tp', axis=0, tiled=True)]
    all_to_all x16 -> x0, waiting for transfers between devices: 103 us -> none  [the longest x4 35.2 us: shards(): lax.all_to_all(projected[:, query_cols + key_cols:], 'tp', split_axis=0,...]
    all_to_all x16 -> x0, starting transfers between devices: 80.1 us -> none  [the longest x4 25.1 us: shards(): lax.all_to_all(projected[:, query_cols:query_cols + key_cols], 'tp', spli...]
    pallas_call x0 -> x1, Pallas kernels: none -> 72.5 us  [shards(): pl.pallas_call(body, out_shape=(jax.ShapeDtypeStruct((4, 16, 512), BF16),...]
    dot_general x22 -> x0, matrix products: 37.8 us -> none  [the longest x4 14.2 us: shards(): jnp.dot(lax.all_gather(hidden[step_index], 'tp', axis=0, tiled=True), mer...]
    unnamed x81 -> x21, local copies, waits for them, and re-layouts: 20.7 us -> 10.5 us
    another operation x11 -> x0, local copies, waits for them, and re-layouts: 6.44 us -> none
    convert_element_type x13 -> x1, other arithmetic: 5.75 us -> 0.01 us  [shards(): angles = positions.astype(F32)[:, None] * frequency]
  transfers between devices with their start and end apart: 17 -> 0, of which waited for: 16 -> 0; matrix products, arithmetic and copies ran while one was open for 12% -> 0% of each run, Pallas kernels for 0% -> 0%
where the time goes in v1:
time: 84.9 us; the launch traced here: 84.6 us
  Pallas kernels  72.5 us (85%)
  local copies, waits for them, and re-layouts  10.5 us (12%)
  between operations  1.31 us (2%)
    pallas_call x1, Pallas kernels, shards(): pl.pallas_call(body, out_shape=(jax.ShapeDtypeStruct((4, 16, 512), BF16),...  72.5 us
    unnamed x21, local copies, waits for them, and re-layouts  10.5 us

profile of v1, /device:TPU:1, one launch (start us, length us, event | category | flops | bytes accessed | tf_op | source)
XLA Modules:
  0.0 84.6 jit_solution(1691318990142705084)
XLA Ops:
  1.3 0.1 fusion
  1.4 0.1 pad_maximum_fusion
  1.5 0.0 copy-start
  1.5 1.4 %copy-done = bf16[1,1536,512]{2,1,0:T(8,128)(2,1)S(1)} copy-done((bf16[1,1536,512]{2,1,0:T(8,128)(2,1)S(1)}, bf16[1,1536,512]{2,1,0:T(8,128)(2,1)}, u32[]{:S(2)}) %copy-start) | copy-done | bytes 1572888
  2.9 0.0 copy-start.1
  2.9 1.4 %copy-done.1 = bf16[1,1536,512]{2,1,0:T(8,128)(2,1)S(1)} copy-done((bf16[1,1536,512]{2,1,0:T(8,128)(2,1)S(1)}, bf16[1,1536,512]{2,1,0:T(8,128)(2,1)}, u32[]{:S(2)}) %copy-start.1) | copy-done | bytes 1572888
  4.3 0.0 copy-start.2
  4.3 1.0 %copy-done.2 = bf16[8192,32]{0,1:T(8,128)(2,1)S(1)} copy-done((bf16[8192,32]{0,1:T(8,128)(2,1)S(1)}, bf16[8192,32]{0,1:T(8,128)(2,1)}, u32[]{:S(2)}) %copy-start.2) | copy-done | bytes 524312
  5.4 0.0 copy-start.3
  5.4 1.0 %copy-done.3 = bf16[8192,32]{0,1:T(8,128)(2,1)S(1)} copy-done((bf16[8192,32]{0,1:T(8,128)(2,1)S(1)}, bf16[8192,32]{0,1:T(8,128)(2,1)}, u32[]{:S(2)}) %copy-start.3) | copy-done | bytes 524312
  6.4 0.0 copy-start.4
  6.4 0.9 %copy-done.4 = bf16[3,512,64]{1,2,0:T(8,128)(2,1)S(1)} copy-done((bf16[3,512,64]{1,2,0:T(8,128)(2,1)S(1)}, bf16[3,512,64]{1,2,0:T(8,128)(2,1)}, u32[]{:S(2)}) %copy-start.4) | copy-done | bytes 196632
  7.3 0.0 copy-start.5
  7.3 0.8 copy-done.5
  8.2 0.0 copy-start.6
  8.2 0.7 copy-done.6
  8.9 0.0 copy-start.7
  8.9 0.7 copy-done.7
  9.5 0.0 copy-start.8
  9.5 0.7 copy-done.8
  10.2 72.5 %shard_map.130 = (bf16[4,16,512]{2,1,0:T(8,128)(2,1)S(1)}, bf16[4,512]{1,0:T(4,128)(2,1)S(1)}, bf16[4,512]{1,0:T(4,128)(2,1)S(1)}) custom-call(s32[1]{0:T(128)} %copy.17.lengths_ref, bf16[4,8192]{1,0:T(4,128)(2,1)S(1)} %bitcast.17, bf16[8192,512]{1,0:T(8,128)(2,1)} %wq_ref.1, bf16[32,8192]{1,0:T(8,128)(2,1)S(1)} %bitcast.14, bf16[32,8192]{1,0:T(8,128)(2,1)S(1)} %bitcast.15, ...), custom_call_target="tpu_custom_call" | custom-call | tf_op jit(solution)/shard_map/pallas_call | solution.py:486
  82.8 0.6 copy.18
  83.4 0.6 copy.19
  84.0 0.6 copy.20
  (2 shorter events, 0.0 us)
Async XLA Ops:
  1.5 1.4 %copy-start = (bf16[1,1536,512]{2,1,0:T(8,128)(2,1)S(1)}, bf16[1,1536,512]{2,1,0:T(8,128)(2,1)}, u32[]{:S(2)}) copy-start(bf16[1,1536,512]{2,1,0:T(8,128)(2,1)} %param.19) | copy-start | bytes 4718596
  2.9 1.4 %copy-start.1 = (bf16[1,1536,512]{2,1,0:T(8,128)(2,1)S(1)}, bf16[1,1536,512]{2,1,0:T(8,128)(2,1)}, u32[]{:S(2)}) copy-start(bf16[1,1536,512]{2,1,0:T(8,128)(2,1)} %param.20) | copy-start | bytes 4718596
  4.3 1.0 %copy-start.2 = (bf16[8192,32]{0,1:T(8,128)(2,1)S(1)}, bf16[8192,32]{0,1:T(8,128)(2,1)}, u32[]{:S(2)}) copy-start(bf16[8192,32]{0,1:T(8,128)(2,1)} %param.13) | copy-start | bytes 1572868
  5.4 1.0 %copy-start.3 = (bf16[8192,32]{0,1:T(8,128)(2,1)S(1)}, bf16[8192,32]{0,1:T(8,128)(2,1)}, u32[]{:S(2)}) copy-start(bf16[8192,32]{0,1:T(8,128)(2,1)} %param.14) | copy-start | bytes 1572868
  6.4 0.9 %copy-start.4 = (bf16[3,512,64]{1,2,0:T(8,128)(2,1)S(1)}, bf16[3,512,64]{1,2,0:T(8,128)(2,1)}, u32[]{:S(2)}) copy-start(bf16[3,512,64]{1,2,0:T(8,128)(2,1)} %param.15) | copy-start | bytes 589828
  7.3 0.8 copy-start.5
  8.2 0.7 copy-start.6
  8.9 0.7 copy-start.7
  9.5 0.7 copy-start.8

commit v2 on v1

v2 whole, which is shorter than its diff:
```python
import functools
import math

import jax
import jax.numpy as jnp
from jax import lax
from jax.experimental import pallas as pl
from jax.experimental.pallas import tpu as pltpu
from jax.sharding import PartitionSpec as P

HEAD_DIM = 128
STEPS = 4
THETA = 500000.0
SCALE = 0.5
MESH = pl.DeviceIdType.MESH
F32 = jnp.float32
BF16 = jnp.bfloat16

SLOTS = 1536
LAG, ES, EL, EH = 3, 6, 11, 15
KEYS = SLOTS + 128
WIDTH = 8192
HALF = WIDTH // 2


def offset(index):
    return (index * (index + 1) // 2) % 4


def body(
    lengths_ref, hidden_ref, wq_ref, wk_ref, wv_ref, a_ref, bq_ref, bk_ref, bv_ref,
    keys_ref, values_ref, tables_ref,
    out_ref, new_keys_ref, new_values_ref,
    length_in, hidden_in, bq_in, bk_in, bv_in, wq, wkv, a_buf, h_buf, k_buf, v_buf,
    b_f32, b_send, b_recv, b_query, b_kv,
    h_f32, h_raw, g_f32,
    a_kv, l_f32, l_send, l_recv, p_send, p_recv, t_all, low_f32,
    acc_q, acc_kv, q_f32, q_send, q_recv, o_send, o_recv, o_f32,
    local_sem, b_ssem, b_rsem, z_ssem, h_rsem, x_ssem, hs_ssem, hs_rsem,
    f_ssem, s_ssem, far_ssem, a_rsem, sib_ssem, sib_rsem,
    l_ssem, l_rsem, p_ssem, p_rsem, t_ssem, t_rsem,
    q_ssem, q_rsem, o_ssem, o_rsem,
):
    r = lax.axis_index("rep")
    t = lax.axis_index("tp")
    y, zl = r // 4, r % 4
    zh, x, c = t // 8, (t // 2) % 4, t % 2
    z = zh * 4 + zl
    other = 1 - c

    def tp_of(high, at_x, core):
        return (high * 4 + at_x) * 2 + core

    def z_step(delta):
        to = (z + 8 + delta) % 8
        return y * 4 + to % 4, tp_of(to // 4, x, c)

    def y_step(delta):
        return ((y + 4 + delta) % 4) * 4 + zl, t

    def pick(first):
        devices = []
        for delta in (1, -1, 2, -2):
            zr, zt = z_step(delta)
            yr, yt = y_step(delta)
            is_y = c if first else other
            devices.append((is_y * yr + (1 - is_y) * zr, is_y * yt + (1 - is_y) * zt))
        return devices

    f_plus, f_minus, f_plus2, f_minus2 = pick(True)
    s_plus, s_minus, s_plus2, s_minus2 = pick(False)
    sibling = (r, tp_of(zh, x, other))

    def origin(core, slot):
        df, ds = offset(slot // 4), offset(slot % 4)
        at_y = (y + core * df + (1 - core) * ds) % 4
        at_z = (zl + (1 - core) * df + core * ds) % 4
        return at_y * 4 + at_z

    def remote(src, dst, ssem, rsem, device):
        return pltpu.make_async_remote_copy(
            src_ref=src, dst_ref=dst, send_sem=ssem, recv_sem=rsem,
            device_id=device, device_id_type=MESH,
        )

    small = [
        pltpu.make_async_copy(source, target, local_sem.at[7 + at])
        for at, (source, target) in enumerate((
            (bq_ref, bq_in), (bk_ref, bk_in), (bv_ref, bv_in), (hidden_ref, hidden_in),
            (lengths_ref, length_in),
        ))
    ]
    loads = [
        pltpu.make_async_copy(a_ref.at[pl.ds(0, 64), pl.ds(0, 256)], a_buf.at[r, 0], local_sem.at[0]),
        pltpu.make_async_copy(a_ref.at[pl.ds(0, 64), pl.ds(256, 256)], a_buf.at[r, 1], local_sem.at[1]),
        pltpu.make_async_copy(wq_ref, wq, local_sem.at[2]),
        pltpu.make_async_copy(wk_ref, wkv.at[pl.ds(0, 32)], local_sem.at[3]),
        pltpu.make_async_copy(wv_ref, wkv.at[pl.ds(32, 32)], local_sem.at[4]),
        pltpu.make_async_copy(keys_ref, k_buf.at[pl.ds(0, SLOTS)], local_sem.at[5]),
        pltpu.make_async_copy(values_ref, v_buf.at[pl.ds(0, SLOTS)], local_sem.at[6]),
        pltpu.make_async_copy(a_ref.at[pl.ds(64, 128)], a_kv, local_sem.at[12]),
    ]
    for load in small + loads:
        load.start()

    barrier = pltpu.get_barrier_semaphore()

    def greet(step, _):
        pl.semaphore_signal(barrier, inc=1, device_id=(r, (t + step) % 16), device_id_type=MESH)
        pl.semaphore_signal(barrier, inc=1, device_id=((r + step) % 16, t), device_id_type=MESH)
        return 0

    lax.fori_loop(1, 16, greet, 0)
    for delta in (1, -1, 2, -2):
        pl.semaphore_signal(barrier, inc=1, device_id=z_step(delta), device_id_type=MESH)

    b_f32[...] = jnp.zeros_like(b_f32)
    for load in small[:4]:
        load.wait()
    up = bq_in[...].astype(F32)
    up_key = bk_in[...].astype(F32)
    up_value = bv_in[...].astype(F32)
    for k in range(4):
        for h in range(4):
            b_f32[8 * k + h : 8 * k + h + 1, :] = up[k : k + 1, 128 * h : 128 * h + 128]
        b_f32[8 * k + 4 : 8 * k + 5, 0:32] = up_key[k : k + 1, :]
        b_f32[8 * k + 5 : 8 * k + 6, 0:32] = up_value[k : k + 1, :]
    b_send[...] = b_f32[0:32, :].astype(BF16)
    own = hidden_in[...].astype(F32)
    for half in range(2):
        for block in range(4):
            start = HALF * half + 1024 * block
            h_f32[half, 4 * block : 4 * block + 4, :] = own[:, start : start + 1024]
    h_raw[t] = h_f32[...].astype(BF16)
    for to in range(16):
        for block in range(4):
            start = 512 * to + 128 * block
            l_f32[to, 4 * block : 4 * block + 4, :] = own[:, start : start + 128]
    l_send[...] = l_f32[...].astype(BF16)
    k_buf[SLOTS:, :] = jnp.zeros((128, 512), BF16)
    v_buf[SLOTS:, :] = jnp.zeros((128, 512), BF16)
    loads[0].wait()
    loads[1].wait()
    pl.semaphore_wait(barrier, 34)

    def held(slot, core):
        return h_raw.at[tp_of((zh + slot // 4) % 2, (x + slot) % 4, core)]

    def z_copy(half):
        block = held(0, c).at[half]
        return remote(
            block, block, z_ssem.at[half], h_rsem.at[4 + half, 0], (r, tp_of(1 - zh, x, c))
        )

    def x_copy(part, way):
        block = held(0, c) if part == 0 else held(4, c).at[part - 1]
        return remote(
            block, block, x_ssem.at[part, way], h_rsem.at[3 + part if part else 0, 4 - way],
            (r, tp_of(zh, (x + way) % 4, c)),
        )

    def hs_copy(slot):
        block = held(slot, c)
        return remote(block, block, hs_ssem.at[slot], hs_rsem.at[slot], sibling)

    def h_in(part, way):
        block = held(way, c) if part == 0 else held(4 + way, c).at[part - 1]
        return remote(
            block, block, hs_ssem.at[0], h_rsem.at[3 + part if part else 0, way], sibling
        )

    def hs_in(slot):
        block = held(slot, other)
        return remote(block, block, hs_ssem.at[slot], hs_rsem.at[slot], sibling)

    def arrange(quad):
        for k in range(4):
            for half in range(2):
                got = h_raw[4 * quad + k, half].astype(F32)
                for block in range(4):
                    start = HALF * half + 1024 * block
                    g_f32[4 * k : 4 * k + 4, start : start + 1024] = got[4 * block : 4 * block + 4, :]
        h_buf[quad] = g_f32[...].astype(BF16)

    def b_copy(step):
        return remote(b_send, b_recv.at[r], b_ssem.at[step], b_rsem.at[step], ((r + step) % 16, t))

    def start_b(step, _):
        b_copy(step).start()
        return 0

    def f_copy(kind):
        if kind < 2:
            mine = a_buf.at[r, c]
            return remote(
                mine, mine, f_ssem.at[kind], a_rsem.at[8 - 4 * kind, 0], (f_plus, f_minus)[kind]
            )
        part = a_buf.at[r, c, pl.ds(32 * (kind - 2), 32)]
        return remote(
            part, part, f_ssem.at[kind], a_rsem.at[12, kind - 2], (f_plus2, f_minus2)[kind - 2]
        )

    def s_copy(index, way):
        chunk = a_buf.at[origin(c, index * 4), c]
        return remote(
            chunk, chunk, s_ssem.at[index, way], a_rsem.at[index * 4 + 2 - way, 0],
            s_plus if way == 0 else s_minus,
        )

    def far_copy(index, way):
        part = a_buf.at[origin(c, index * 4), c, pl.ds(32 * way, 32)]
        return remote(
            part, part, far_ssem.at[index, way], a_rsem.at[index * 4 + 3, way],
            s_plus2 if way == 0 else s_minus2,
        )

    def s_start(index):
        s_copy(index, 0).start()
        s_copy(index, 1).start()
        far_copy(index, 0).start()
        far_copy(index, 1).start()

    def sib_copy(slot):
        chunk = a_buf.at[origin(c, slot), c]
        return remote(chunk, chunk, sib_ssem.at[slot], sib_rsem.at[slot], sibling)

    def sib_in(slot):
        chunk = a_buf.at[origin(other, slot), other]
        return remote(chunk, chunk, sib_ssem.at[slot], sib_rsem.at[slot], sibling)

    def a_in(slot, part=None):
        chunk = a_buf.at[origin(c, slot), c]
        if part is not None:
            chunk = chunk.at[pl.ds(32 * part, 32)]
        return remote(
            chunk, chunk, sib_ssem.at[slot], a_rsem.at[slot, 0 if part is None else part], sibling
        )

    def l_copy(step):
        to = (r + step) % 16
        return remote(l_send.at[to], l_recv.at[r], l_ssem.at[step], l_rsem.at[step], (to, t))

    def p_copy(step):
        to = (r + step) % 16
        return remote(p_send.at[to], p_recv.at[r], p_ssem.at[step], p_rsem.at[step], (to, t))

    def t_copy(step):
        to = (t + step) % 16
        return remote(t_all.at[t], t_all.at[t], t_ssem.at[step], t_rsem.at[step], (r, to))

    def t_in(step):
        block = t_all.at[(t + 16 - step) % 16]
        return remote(block, block, t_ssem.at[step], t_rsem.at[step], (r, (t + step) % 16))

    def each(copy, what):
        def one(step, _):
            if what == "start":
                copy(step).start()
            elif what == "wait_recv":
                copy(step).wait_recv()
            else:
                copy(step).wait_send()
            return 0

        lax.fori_loop(1, 16, one, 0)

    each(l_copy, "start")
    z_copy(0).start()
    z_copy(1).start()
    for way in (2, 1, 3):
        x_copy(0, way).start()
    each(b_copy, "start")
    for k in range(4):
        f_copy(k).start()
    hs_copy(0).start()
    s_start(0)
    b_recv[r] = b_send[...]
    l_recv[r] = l_send[r]
    loads[7].wait()

    for index in (1, 2):
        a_in(4 * index).wait_recv()
        s_start(index)
        sib_copy(4 * index).start()
    a_in(12, 0).wait_recv()
    a_in(12, 1).wait_recv()
    s_start(3)
    sib_copy(12).start()
    each(l_copy, "wait_recv")
    slices = l_recv[...].reshape(256, 128)
    block_of = (lax.broadcasted_iota(jnp.int32, (256, 128), 0) // 4) % 4
    sums = jnp.zeros((256, 128), F32)
    for block in range(4):
        sums += lax.dot_general(
            jnp.where(block_of == block, slices, jnp.zeros_like(slices)),
            a_kv[:, 128 * block : 128 * block + 128],
            (((1,), (1,)), ((), ())), preferred_element_type=F32,
        )
    sums = sums.reshape(16, 2, 8, 128)
    p_send[...] = sums[:, 0] + sums[:, 1]
    each(p_copy, "start")
    p_recv[r] = p_send[r]
    for k in (1, 3, 2):
        h_in(0, k).wait_recv()
        hs_copy(k).start()
    h_in(1, 0).wait_recv()
    for to in (2, 1, 3):
        x_copy(1, to).start()

    def wait_b(step, _):
        b_copy(step).wait_recv()
        return 0

    lax.fori_loop(1, 16, wait_b, 0)
    b_f32[...] = b_recv[...].reshape(512, 128).astype(F32)
    for h in range(4):
        b_query[:, 128 * h : 128 * h + 128] = (SCALE * b_f32[pl.ds(h, 64, stride=8), :]).astype(BF16)
    bk_all = SCALE * b_f32[pl.ds(4, 64, stride=8), :]
    bv_all = SCALE * b_f32[pl.ds(5, 64, stride=8), :]
    b_kv[0:64, :] = bk_all.astype(BF16)
    b_kv[64:128, :] = pltpu.roll(bv_all, 32, 1).astype(BF16)

    acc_q[...] = jnp.zeros_like(acc_q)
    acc_kv[...] = jnp.zeros_like(acc_kv)
    for load in loads[2:5]:
        load.wait()

    def merge(at, half):
        start = pl.multiple_of(at * 512 + half * 256, 256)
        down = a_buf[at, half]
        low = lax.dot_general(
            down, b_query[...], (((0,), (0,)), ((), ())), preferred_element_type=F32
        )
        rows = pl.ds(start, 256)
        wq[rows, :] = (wq[rows, :].astype(F32) + low).astype(BF16)

    def project(part):
        start = pl.multiple_of(part * 2048, 2048)
        states = h_buf[:, :, pl.ds(start, 2048)].reshape(64, 2048)
        acc_q[...] += jnp.dot(states, wq[pl.ds(start, 2048), :], preferred_element_type=F32)
        acc_kv[...] += lax.dot_general(
            states, wkv[:, pl.ds(start, 2048)], (((1,), (1,)), ((), ())), preferred_element_type=F32
        )

    def slot_at(at):
        phase, m = at // 4, at % 4
        middle = ((phase + 1) // 2) % 2
        return middle * (8 * (phase - 1) + 4 * (m // 2) + 1 + m % 2) + (1 - middle) * (4 * m + phase)

    def first(at, _):
        merge(origin(c, slot_at(at)), c)
        return 0

    lax.fori_loop(0, LAG, first, 0)
    h_in(2, 0).wait_recv()
    for to in (2, 1, 3):
        x_copy(2, to).start()
    hs_copy(4).start()

    def turn(at, _):
        slot = slot_at(at)

        @pl.when((at > 3) & (at < 12))
        def _():
            a_in(slot).wait_recv()
            sib_copy(slot).start()

        @pl.when(at >= 12)
        def _():
            a_in(slot, 0).wait_recv()
            a_in(slot, 1).wait_recv()
            sib_copy(slot).start()

        @pl.when(at == ES)
        def _():
            for k in range(4):
                hs_in(k).wait_recv()
            for k in range(2):
                arrange(2 * zh + k)

        @pl.when(at == EL)
        def _():
            each(p_copy, "wait_recv")
            total = jnp.sum(p_recv[...], 0)
            t_all[t] = total + pltpu.roll(total, 4, 0)
            each(t_copy, "start")

        @pl.when(at == EH)
        def _():
            for k in (1, 3, 2):
                h_in(1, k).wait_recv()
                h_in(2, k).wait_recv()
                hs_copy(4 + k).start()

        late = slot_at(at - LAG)

        @pl.when(at > LAG)
        def _():
            sib_in(late).wait_recv()

        merge(origin(c, slot), c)
        merge(origin(other, late), other)
        return 0

    lax.fori_loop(LAG, 16, turn, 0)

    def last(at, _):
        sib_in(slot_at(at)).wait_recv()
        merge(origin(other, slot_at(at)), other)
        return 0

    lax.fori_loop(16 - LAG, 16, last, 0)
    for k in range(4, 8):
        hs_in(k).wait_recv()
    for k in range(2):
        arrange(2 * (1 - zh) + k)

    def project_turn(part, _):
        project(part)
        return 0

    lax.fori_loop(0, 4, project_turn, 0)
    each(t_in, "wait_recv")
    low_in = t_all[...].reshape(128, 128)
    low_high = low_in.astype(BF16)
    low_rest = (low_in - low_high.astype(F32)).astype(BF16)
    low = jnp.dot(low_high, b_kv[...], preferred_element_type=F32) + jnp.dot(
        low_rest, b_kv[...], preferred_element_type=F32
    )
    for to in range(16):
        low_f32[4 * to : 4 * to + 4, :] = low[8 * to : 8 * to + 4, :]

    acc = acc_q[...]
    kv = jnp.concatenate([acc_kv[...], jnp.zeros((64, 64), F32)], 1) + low_f32[...]
    lane = lax.broadcasted_iota(jnp.int32, (64, 128), 1)
    mine = lane // 32 == t % 4
    own_key = jnp.where(mine, pltpu.roll(kv, (t % 4) * 32, 1), 0.0)
    own_value = jnp.where(mine, pltpu.roll(kv, (t % 4) * 32 + 96, 1), 0.0)
    for to in range(16):
        base = 4 * to
        for h in range(4):
            q_f32[to, 4 * h : 4 * h + 4, :] = acc[base : base + 4, 128 * h : 128 * h + 128]
        q_f32[to, 16:20, :] = own_key[base : base + 4]
        q_f32[to, 20:24, :] = own_value[base : base + 4]
        q_f32[to, 24:32, :] = jnp.zeros((8, 128), F32)
    q_send[...] = q_f32[...].astype(BF16)

    def q_copy(step):
        to = (t + step) % 16
        return remote(q_send.at[to], q_recv.at[t], q_ssem.at[step], q_rsem.at[step], (r, to))

    def start_q(step, _):
        q_copy(step).start()
        return 0

    lax.fori_loop(1, 16, start_q, 0)
    q_recv[t] = q_send[t]
    loads[5].wait()
    loads[6].wait()

    each(b_copy, "wait_send")
    each(sib_copy, "wait_send")
    each(l_copy, "wait_send")
    each(p_copy, "wait_send")
    each(t_copy, "wait_send")
    for half in range(2):
        z_copy(half).wait_send()
    for slot in range(8):
        hs_copy(slot).wait_send()
    for part in range(3):
        for way in range(1, 4):
            x_copy(part, way).wait_send()
    for k in range(4):
        f_copy(k).wait_send()
        for way in range(2):
            s_copy(k, way).wait_send()
            far_copy(k, way).wait_send()

    def wait_q(step, _):
        q_copy(step).wait_recv()
        return 0

    lax.fori_loop(1, 16, wait_q, 0)

    small[4].wait()
    cosine, sine = tables_ref[0], tables_ref[1]
    length = length_in[0]
    column = lax.broadcasted_iota(jnp.int32, (64, KEYS), 1)
    step_of = lax.broadcasted_iota(jnp.int32, (64, KEYS), 0) % 4
    valid = (column < length) | ((column >= SLOTS) & (column - SLOTS <= step_of))
    scaling = 1.0 / math.sqrt(HEAD_DIM)

    def rotated(values, cos_rows, sin_rows):
        return values * cos_rows + pltpu.roll(values, 64, values.ndim - 1) * sin_rows

    def o_copy(step):
        to = (t + step) % 16
        return remote(o_send.at[to], o_recv.at[t], o_ssem.at[step], o_rsem.at[step], (r, to))

    def start_o(step, _):
        o_copy(step).start()
        return 0

    for g in range(4):
        cols = slice(128 * g, 128 * g + 128)
        fresh = q_recv[4 * g, 16:32, :].astype(F32)
        for u in range(1, 4):
            fresh += q_recv[4 * g + u, 16:32, :].astype(F32)
        fresh_key = rotated(fresh, cosine, sine)[0:4].astype(BF16)
        fresh_value = fresh[4:8].astype(BF16)
        new_keys_ref[:, cols] = fresh_key
        new_values_ref[:, cols] = fresh_value
        pad = jnp.zeros((12, 128), BF16)
        k_buf[SLOTS : SLOTS + 16, cols] = jnp.concatenate([fresh_key, pad], 0)
        v_buf[SLOTS : SLOTS + 16, cols] = jnp.concatenate([fresh_value, pad], 0)
        query = q_recv[4 * g : 4 * g + 4, 0:16, :].astype(F32).reshape(64, 128)
        tables = (jnp.concatenate([cosine] * 4, 0), jnp.concatenate([sine] * 4, 0))
        query = rotated(query, *tables).astype(BF16)
        scores = scaling * lax.dot_general(
            query, k_buf[:, cols], (((1,), (1,)), ((), ())), preferred_element_type=F32
        )
        scores = jnp.where(valid, scores, -1e30)
        highest = jnp.max(scores, -1, keepdims=True)
        weights = jnp.where(valid, jnp.exp(scores - highest), 0.0)
        total = jnp.sum(weights, -1, keepdims=True)
        probs = (weights * (1.0 / total)).astype(BF16)
        blended = jnp.dot(probs, v_buf[:, cols], preferred_element_type=F32).astype(BF16)
        o_send[4 * g : 4 * g + 4] = blended.reshape(4, 16, 128)

    lax.fori_loop(1, 16, start_o, 0)
    o_recv[t] = o_send[t]

    def wait_q_sends(step, _):
        q_copy(step).wait_send()
        return 0

    lax.fori_loop(1, 16, wait_q_sends, 0)

    def wait_o(step, _):
        o_copy(step).wait_recv()
        return 0

    lax.fori_loop(1, 16, wait_o, 0)
    o_f32[...] = o_recv[...].reshape(256, 128).astype(F32)
    for s in range(STEPS):
        for h in range(4):
            out_ref[s, :, 128 * h : 128 * h + 128] = o_f32[
                pl.ds(4 * h + s, 16, stride=16), :
            ].astype(BF16)

    def wait_last(step, _):
        o_copy(step).wait_send()
        return 0

    lax.fori_loop(1, 16, wait_last, 0)


def shards(
    hidden, w_query, w_key, w_value, a_factors, b_query, b_key, b_value,
    key_cache, value_cache, lengths,
):
    half_dim = HEAD_DIM // 2
    frequency = THETA ** (-(jnp.arange(half_dim, dtype=F32) * 2.0 / HEAD_DIM))
    positions = lengths[0] + jnp.arange(16, dtype=jnp.int32) % STEPS
    angles = positions.astype(F32)[:, None] * frequency
    cosine, sine = jnp.cos(angles), jnp.sin(angles)
    tables = jnp.stack(
        [jnp.concatenate([cosine, cosine], 1), jnp.concatenate([-sine, sine], 1)]
    )

    anywhere = pl.BlockSpec(memory_space=pltpu.HBM)
    vmem = pl.BlockSpec(memory_space=pltpu.VMEM)
    dma = pltpu.SemaphoreType.DMA
    attended, new_keys, new_values = pl.pallas_call(
        body,
        out_shape=(
            pltpu.VMEM((4, 16, 512), BF16),
            pltpu.VMEM((4, 512), BF16),
            pltpu.VMEM((4, 512), BF16),
        ),
        in_specs=[anywhere] * 11 + [vmem],
        out_specs=(vmem, vmem, vmem),
        scratch_shapes=[
            pltpu.SMEM((1,), jnp.int32),
            pltpu.VMEM((4, WIDTH), BF16),
            pltpu.VMEM((4, 512), BF16),
            pltpu.VMEM((4, 32), BF16),
            pltpu.VMEM((4, 32), BF16),
            pltpu.VMEM((WIDTH, 512), BF16),
            pltpu.VMEM((64, WIDTH), BF16),
            pltpu.VMEM((16, 2, 64, 256), BF16),
            pltpu.VMEM((4, 16, WIDTH), BF16),
            pltpu.VMEM((KEYS, 512), BF16),
            pltpu.VMEM((KEYS, 512), BF16),
            pltpu.VMEM((512, 128), F32),
            pltpu.VMEM((32, 128), BF16),
            pltpu.VMEM((16, 32, 128), BF16),
            pltpu.VMEM((64, 512), BF16),
            pltpu.VMEM((128, 128), BF16),
            pltpu.VMEM((2, 16, 1024), F32),
            pltpu.VMEM((16, 2, 16, 1024), BF16),
            pltpu.VMEM((16, WIDTH), F32),
            pltpu.VMEM((128, 512), BF16),
            pltpu.VMEM((16, 16, 128), F32),
            pltpu.VMEM((16, 16, 128), BF16),
            pltpu.VMEM((16, 16, 128), BF16),
            pltpu.VMEM((16, 8, 128), F32),
            pltpu.VMEM((16, 8, 128), F32),
            pltpu.VMEM((16, 8, 128), F32),
            pltpu.VMEM((64, 128), F32),
            pltpu.VMEM((64, 512), F32),
            pltpu.VMEM((64, 64), F32),
            pltpu.VMEM((16, 32, 128), F32),
            pltpu.VMEM((16, 32, 128), BF16),
            pltpu.VMEM((16, 32, 128), BF16),
            pltpu.VMEM((16, 16, 128), BF16),
            pltpu.VMEM((16, 16, 128), BF16),
            pltpu.VMEM((256, 128), F32),
            dma((13,)), dma((16,)), dma((16,)), dma((2,)), dma((6, 4)),
            dma((3, 4)), dma((8,)), dma((8,)),
            dma((4,)), dma((4, 2)), dma((4, 2)), dma((16, 2)), dma((16,)), dma((16,)),
            dma((16,)), dma((16,)), dma((16,)), dma((16,)), dma((16,)), dma((16,)),
            dma((16,)), dma((16,)), dma((16,)), dma((16,)),
        ],
        compiler_params=pltpu.CompilerParams(
            collective_id=0, has_side_effects=True, vmem_limit_bytes=62 * 1024 * 1024
        ),
    )(
        lengths, hidden[:, 0], w_query, w_key.T, w_value.T,
        jnp.swapaxes(a_factors, 1, 2).reshape(192, 512), b_query, b_key, b_value,
        key_cache[0], value_cache[0], tables,
    )
    return attended, new_keys[:, None], new_values[:, None]


def solution(mesh):
    placed = (
        P(None, ("rep", "tp"), None),
        P(None, "tp"),
        P(None, "tp"),
        P(None, "tp"),
        P(None, "rep", None),
        P("rep", "tp"),
        P("rep", "tp"),
        P("rep", "tp"),
        P(("rep", "tp"), None, None),
        P(("rep", "tp"), None, None),
        P(("rep", "tp")),
    )
    return jax.shard_map(
        shards,
        mesh=mesh,
        in_specs=placed,
        out_specs=(
            P(None, "rep", "tp"),
            P(None, ("rep", "tp"), None),
            P(None, ("rep", "tp"), None),
        ),
        check_vma=False,
    )
```

time: 84.9 us -> 59.2 us (0.70)
  Pallas kernels: 72.5 us -> 55 us
  local copies, waits for them, and re-layouts: 10.5 us -> 1.82 us
    pallas_call x1, Pallas kernels: 72.5 us -> 55 us  [shards(): pl.pallas_call(body, out_shape=(pltpu.VMEM((4, 16, 512), BF16), pltpu.VME...]
    unnamed x21 -> x3, local copies, waits for them, and re-layouts: 10.5 us -> 1.82 us
where the time goes in v2:
time: 59.2 us; the launch traced here: 59 us
  Pallas kernels  55 us (93%)
  local copies, waits for them, and re-layouts  1.82 us (3%)
  between operations  1.3 us (2%)
  other arithmetic  0.82 us (1%)
    pallas_call x1, Pallas kernels, shards(): pl.pallas_call(body, out_shape=(pltpu.VMEM((4, 16, 512), BF16), pltpu.VME...  55 us
    unnamed x3, local copies, waits for them, and re-layouts  1.82 us

profile of v2, /device:TPU:1, one launch (start us, length us, event | category | flops | bytes accessed | tf_op | source)
XLA Modules:
  0.0 59.0 jit_solution(15822277010929102441)
XLA Ops:
  1.3 0.1 multiply_cosine_fusion
  1.4 0.1 maximum_bitcast_fusion
  1.5 0.6 %pad_maximum_fusion.tables_ref = f32[2,16,128]{2,1,0:T(8,128)} fusion(f32[1,16,128]{2,1,0:T(8,128)S(1)} %get-tuple-element.13, f32[1,16,128]{2,1,0:T(8,128)S(1)} %get-tuple-element.12), kind=kLoop, calls=%fused_computation | loop fusion | flops 4096 | bytes 32768 | tf_op jit(solution)/shard_map/stack | solution.py:567
  2.1 55.0 %shard_map.130 = (bf16[4,16,512]{2,1,0:T(8,128)(2,1)S(1)}, bf16[4,512]{1,0:T(4,128)(2,1)S(1)}, bf16[4,512]{1,0:T(4,128)(2,1)S(1)}) custom-call(s32[1]{0:T(128)} %copy.20.lengths_ref, bf16[4,8192]{1,0:T(4,128)(2,1)} %bitcast.23, bf16[8192,512]{1,0:T(8,128)(2,1)} %wq_ref.1, bf16[32,8192]{1,0:T(8,128)(2,1)} %bitcast.20, bf16[32,8192]{1,0:T(8,128)(2,1)} %bitcast.21, ...), custom_call_target="tpu_custom_call" | custom-call | tf_op jit(solution)/shard_map/pallas_call | solution.py:574
  57.2 0.6 %copy.17 = bf16[4,16,512]{2,1,0:T(8,128)(2,1)} copy(bf16[4,16,512]{2,1,0:T(8,128)(2,1)S(1)} %get-tuple-element.14) | data formatting | bytes 131072
  57.8 0.6 %copy.18 = bf16[4,1,512]{2,0,1:T(4,128)(2,1)} copy(bf16[4,1,512]{2,0,1:T(4,128)(2,1)S(1)} %bitcast.17) | data formatting | bytes 8192
  58.4 0.6 %copy.19 = bf16[4,1,512]{2,0,1:T(4,128)(2,1)} copy(bf16[4,1,512]{2,0,1:T(4,128)(2,1)S(1)} %bitcast.16) | data formatting | bytes 8192
  (2 shorter events, 0.0 us)

commit v3 on v2

--- a/solution.py
+++ b/solution.py
@@ -17,7 +17,7 @@
 BF16 = jnp.bfloat16
 
 SLOTS = 1536
-LAG, ES, EL, EH = 3, 6, 11, 15
+LAG, ES, EW, EH = 3, 6, 10, 15
 KEYS = SLOTS + 128
 WIDTH = 8192
 HALF = WIDTH // 2
@@ -29,16 +29,16 @@
 
 def body(
     lengths_ref, hidden_ref, wq_ref, wk_ref, wv_ref, a_ref, bq_ref, bk_ref, bv_ref,
-    keys_ref, values_ref, tables_ref,
-    out_ref, new_keys_ref, new_values_ref,
-    length_in, hidden_in, bq_in, bk_in, bv_in, wq, wkv, a_buf, h_buf, k_buf, v_buf,
-    b_f32, b_send, b_recv, b_query, b_kv,
+    keys_ref, values_ref,
+    out_ref, fresh_ref,
+    tables, length_in, hidden_in, bq_in, bk_in, bv_in, wq, wkv, a_buf, h_buf, k_buf, v_buf,
+    b_f32, b_send, b_recv, b_query, w_send,
     h_f32, h_raw, g_f32,
-    a_kv, l_f32, l_send, l_recv, p_send, p_recv, t_all, low_f32,
-    acc_q, acc_kv, q_f32, q_send, q_recv, o_send, o_recv, o_f32,
+    a_kv, l_f32, l_send, l_recv, p_send, p_recv, w_recv, low_f32,
+    acc_q, acc_kv, q_f32, q_send, q_recv, n_send, n_recv, o_send, o_recv, o_f32,
     local_sem, b_ssem, b_rsem, z_ssem, h_rsem, x_ssem, hs_ssem, hs_rsem,
     f_ssem, s_ssem, far_ssem, a_rsem, sib_ssem, sib_rsem,
-    l_ssem, l_rsem, p_ssem, p_rsem, t_ssem, t_rsem,
+    l_ssem, l_rsem, p_ssem, p_rsem, w_ssem, w_rsem, n_ssem, n_rsem,
     q_ssem, q_rsem, o_ssem, o_rsem,
 ):
     r = lax.axis_index("rep")
@@ -139,6 +139,13 @@
     l_send[...] = l_f32[...].astype(BF16)
     k_buf[SLOTS:, :] = jnp.zeros((128, 512), BF16)
     v_buf[SLOTS:, :] = jnp.zeros((128, 512), BF16)
+    small[4].wait()
+    lanes = lax.broadcasted_iota(jnp.int32, (16, 128), 1)
+    frequency = jnp.exp((lanes % 64).astype(F32) * (-2.0 * math.log(THETA) / HEAD_DIM))
+    ahead = lax.broadcasted_iota(jnp.int32, (16, 128), 0) % STEPS
+    angles = (length_in[0] + ahead).astype(F32) * frequency
+    tables[0] = jnp.cos(angles)
+    tables[1] = jnp.where(lanes < 64, -jnp.sin(angles), jnp.sin(angles))
     loads[0].wait()
     loads[1].wait()
     pl.semaphore_wait(barrier, 34)
@@ -244,13 +251,9 @@
         to = (r + step) % 16
         return remote(p_send.at[to], p_recv.at[r], p_ssem.at[step], p_rsem.at[step], (to, t))
 
-    def t_copy(step):
+    def w_copy(step):
         to = (t + step) % 16
-        return remote(t_all.at[t], t_all.at[t], t_ssem.at[step], t_rsem.at[step], (r, to))
-
-    def t_in(step):
-        block = t_all.at[(t + 16 - step) % 16]
-        return remote(block, block, t_ssem.at[step], t_rsem.at[step], (r, (t + step) % 16))
+        return remote(w_send, w_recv.at[t], w_ssem.at[step], w_rsem.at[step], (r, to))
 
     def each(copy, what):
         def one(step, _):
@@ -264,14 +267,14 @@
 
         lax.fori_loop(1, 16, one, 0)
 
-    each(l_copy, "start")
     z_copy(0).start()
     z_copy(1).start()
+    for k in range(4):
+        f_copy(k).start()
+    each(b_copy, "start")
     for way in (2, 1, 3):
         x_copy(0, way).start()
-    each(b_copy, "start")
-    for k in range(4):
-        f_copy(k).start()
+    each(l_copy, "start")
     hs_copy(0).start()
     s_start(0)
     b_recv[r] = b_send[...]
@@ -286,6 +289,64 @@
     a_in(12, 1).wait_recv()
     s_start(3)
     sib_copy(12).start()
+    for k in (1, 3, 2):
+        h_in(0, k).wait_recv()
+        hs_copy(k).start()
+    h_in(1, 0).wait_recv()
+    for to in (2, 1, 3):
+        x_copy(1, to).start()
+
+    def wait_b(step, _):
+        b_copy(step).wait_recv()
+        return 0
+
+    lax.fori_loop(1, 16, wait_b, 0)
+    b_f32[...] = b_recv[...].reshape(512, 128).astype(F32)
+    for h in range(4):
+        b_query[:, 128 * h : 128 * h + 128] = (SCALE * b_f32[pl.ds(h, 64, stride=8), :]).astype(BF16)
+    bk_all = SCALE * b_f32[pl.ds(4, 64, stride=8), :]
+    bv_all = SCALE * b_f32[pl.ds(5, 64, stride=8), :]
+    both = bk_all + pltpu.roll(bv_all, 32, 1)
+    w_send[...] = (both[0:32] + pltpu.roll(both[32:64], 64, 1)).astype(BF16)
+    w_recv[t] = w_send[...]
+
+    acc_q[...] = jnp.zeros_like(acc_q)
+    acc_kv[...] = jnp.zeros_like(acc_kv)
+    for load in loads[2:5]:
+        load.wait()
+
+    def merge(at, half):
+        start = pl.multiple_of(at * 512 + half * 256, 256)
+        down = a_buf[at, half]
+        low = lax.dot_general(
+            down, b_query[...], (((0,), (0,)), ((), ())), preferred_element_type=F32
+        )
+        rows = pl.ds(start, 256)
+        wq[rows, :] = (wq[rows, :].astype(F32) + low).astype(BF16)
+
+    def project(part):
+        start = pl.multiple_of(part * 2048, 2048)
+        states = h_buf[:, :, pl.ds(start, 2048)].reshape(64, 2048)
+        acc_q[...] += jnp.dot(states, wq[pl.ds(start, 2048), :], preferred_element_type=F32)
+        acc_kv[...] += lax.dot_general(
+            states, wkv[:, pl.ds(start, 2048)], (((1,), (1,)), ((), ())), preferred_element_type=F32
+        )
+
+    def slot_at(at):
+        phase, m = at // 4, at % 4
+        middle = ((phase + 1) // 2) % 2
+        return middle * (8 * (phase - 1) + 4 * (m // 2) + 1 + m % 2) + (1 - middle) * (4 * m + phase)
+
+    def first(at, _):
+        merge(origin(c, slot_at(at)), c)
+        return 0
+
+    lax.fori_loop(0, LAG, first, 0)
+    h_in(2, 0).wait_recv()
+    for to in (2, 1, 3):
+        x_copy(2, to).start()
+    hs_copy(4).start()
+
     each(l_copy, "wait_recv")
     slices = l_recv[...].reshape(256, 128)
     block_of = (lax.broadcasted_iota(jnp.int32, (256, 128), 0) // 4) % 4
@@ -300,62 +361,6 @@
     p_send[...] = sums[:, 0] + sums[:, 1]
     each(p_copy, "start")
     p_recv[r] = p_send[r]
-    for k in (1, 3, 2):
-        h_in(0, k).wait_recv()
-        hs_copy(k).start()
-    h_in(1, 0).wait_recv()
-    for to in (2, 1, 3):
-        x_copy(1, to).start()
-
-    def wait_b(step, _):
-        b_copy(step).wait_recv()
-        return 0
-
-    lax.fori_loop(1, 16, wait_b, 0)
-    b_f32[...] = b_recv[...].reshape(512, 128).astype(F32)
-    for h in range(4):
-        b_query[:, 128 * h : 128 * h + 128] = (SCALE * b_f32[pl.ds(h, 64, stride=8), :]).astype(BF16)
-    bk_all = SCALE * b_f32[pl.ds(4, 64, stride=8), :]
-    bv_all = SCALE * b_f32[pl.ds(5, 64, stride=8), :]
-    b_kv[0:64, :] = bk_all.astype(BF16)
-    b_kv[64:128, :] = pltpu.roll(bv_all, 32, 1).astype(BF16)
-
-    acc_q[...] = jnp.zeros_like(acc_q)
-    acc_kv[...] = jnp.zeros_like(acc_kv)
-    for load in loads[2:5]:
-        load.wait()
-
-    def merge(at, half):
-        start = pl.multiple_of(at * 512 + half * 256, 256)
-        down = a_buf[at, half]
-        low = lax.dot_general(
-            down, b_query[...], (((0,), (0,)), ((), ())), preferred_element_type=F32
-        )
-        rows = pl.ds(start, 256)
-        wq[rows, :] = (wq[rows, :].astype(F32) + low).astype(BF16)
-
-    def project(part):
-        start = pl.multiple_of(part * 2048, 2048)
-        states = h_buf[:, :, pl.ds(start, 2048)].reshape(64, 2048)
-        acc_q[...] += jnp.dot(states, wq[pl.ds(start, 2048), :], preferred_element_type=F32)
-        acc_kv[...] += lax.dot_general(
-            states, wkv[:, pl.ds(start, 2048)], (((1,), (1,)), ((), ())), preferred_element_type=F32
-        )
-
-    def slot_at(at):
-        phase, m = at // 4, at % 4
-        middle = ((phase + 1) // 2) % 2
-        return middle * (8 * (phase - 1) + 4 * (m // 2) + 1 + m % 2) + (1 - middle) * (4 * m + phase)
-
-    def first(at, _):
-        merge(origin(c, slot_at(at)), c)
-        return 0
-
-    lax.fori_loop(0, LAG, first, 0)
-    h_in(2, 0).wait_recv()
-    for to in (2, 1, 3):
-        x_copy(2, to).start()
-    hs_copy(4).start()
 
     def turn(at, _):
         slot = slot_at(at)
@@ -378,12 +383,9 @@
             for k in range(2):
                 arrange(2 * zh + k)
 
-        @pl.when(at == EL)
+        @pl.when(at == EW)
         def _():
-            each(p_copy, "wait_recv")
-            total = jnp.sum(p_recv[...], 0)
-            t_all[t] = total + pltpu.roll(total, 4, 0)
-            each(t_copy, "start")
+            each(w_copy, "start")
 
         @pl.when(at == EH)
         def _():
@@ -420,18 +422,8 @@
         return 0
 
     lax.fori_loop(0, 4, project_turn, 0)
-    each(t_in, "wait_recv")
-    low_in = t_all[...].reshape(128, 128)
-    low_high = low_in.astype(BF16)
-    low_rest = (low_in - low_high.astype(F32)).astype(BF16)
-    low = jnp.dot(low_high, b_kv[...], preferred_element_type=F32) + jnp.dot(
-        low_rest, b_kv[...], preferred_element_type=F32
-    )
-    for to in range(16):
-        low_f32[4 * to : 4 * to + 4, :] = low[8 * to : 8 * to + 4, :]
-
     acc = acc_q[...]
-    kv = jnp.concatenate([acc_kv[...], jnp.zeros((64, 64), F32)], 1) + low_f32[...]
+    kv = jnp.concatenate([acc_kv[...], jnp.zeros((64, 64), F32)], 1)
     lane = lax.broadcasted_iota(jnp.int32, (64, 128), 1)
     mine = lane // 32 == t % 4
     own_key = jnp.where(mine, pltpu.roll(kv, (t % 4) * 32, 1), 0.0)
@@ -440,21 +432,26 @@
         base = 4 * to
         for h in range(4):
             q_f32[to, 4 * h : 4 * h + 4, :] = acc[base : base + 4, 128 * h : 128 * h + 128]
-        q_f32[to, 16:20, :] = own_key[base : base + 4]
-        q_f32[to, 20:24, :] = own_value[base : base + 4]
-        q_f32[to, 24:32, :] = jnp.zeros((8, 128), F32)
+        n_send[to, 0:4, :] = own_key[base : base + 4]
+        n_send[to, 4:8, :] = own_value[base : base + 4]
     q_send[...] = q_f32[...].astype(BF16)
 
     def q_copy(step):
         to = (t + step) % 16
         return remote(q_send.at[to], q_recv.at[t], q_ssem.at[step], q_rsem.at[step], (r, to))
 
+    def n_copy(step):
+        to = (t + step) % 16
+        return remote(n_send.at[to], n_recv.at[t], n_ssem.at[step], n_rsem.at[step], (r, to))
+
     def start_q(step, _):
         q_copy(step).start()
+        n_copy(step).start()
         return 0
 
     lax.fori_loop(1, 16, start_q, 0)
     q_recv[t] = q_send[t]
+    n_recv[t] = n_send[t]
     loads[5].wait()
     loads[6].wait()
 
@@ -462,7 +459,7 @@
     each(sib_copy, "wait_send")
     each(l_copy, "wait_send")
     each(p_copy, "wait_send")
-    each(t_copy, "wait_send")
+    each(w_copy, "wait_send")
     for half in range(2):
         z_copy(half).wait_send()
     for slot in range(8):
@@ -476,14 +473,44 @@
             s_copy(k, way).wait_send()
             far_copy(k, way).wait_send()
 
+    each(p_copy, "wait_recv")
+    each(w_copy, "wait_recv")
+    total = jnp.sum(p_recv[...], 0)
+    total = total + pltpu.roll(total, 4, 0)
+    total_high = total.astype(BF16).astype(F32)
+    total_rest = total - total_high
+    key_rank = lax.broadcasted_iota(jnp.int32, (8, 128), 1) < 64
+    totals = jnp.concatenate(
+        [
+            jnp.where(key_rank, total_high, 0.0),
+            jnp.where(key_rank, total_rest, 0.0),
+            jnp.where(key_rank, 0.0, total_high),
+            jnp.where(key_rank, 0.0, total_rest),
+        ],
+        0,
+    ).astype(BF16)
+    key_row = lax.broadcasted_iota(jnp.int32, (8, 128), 0) < 4
+    quarter = lax.broadcasted_iota(jnp.int32, (32, 128), 1) // 32
+    for g in range(4):
+        ups = [jnp.zeros((32, 128), F32) for _ in range(4)]
+        for u in range(4):
+            block = w_recv[4 * g + u].astype(F32)
+            for at, held_at in enumerate((0, 2, 1, 3)):
+                shift = (32 * u - 32 * held_at) % 128
+                moved = pltpu.roll(block, shift, 1) if shift else block
+                ups[at] += jnp.where(quarter == u, moved, 0.0)
+        up_all = jnp.concatenate(ups, 0).astype(BF16)
+        low = jnp.dot(totals, up_all, preferred_element_type=F32)
+        low_f32[g] = jnp.where(key_row, low[0:8] + low[8:16], low[16:24] + low[24:32])
+
     def wait_q(step, _):
         q_copy(step).wait_recv()
+        n_copy(step).wait_recv()
         return 0
 
     lax.fori_loop(1, 16, wait_q, 0)
 
-    small[4].wait()
-    cosine, sine = tables_ref[0], tables_ref[1]
+    cosine, sine = tables[0], tables[1]
     length = length_in[0]
     column = lax.broadcasted_iota(jnp.int32, (64, KEYS), 1)
     step_of = lax.broadcasted_iota(jnp.int32, (64, KEYS), 0) % 4
@@ -503,17 +530,16 @@
 
     for g in range(4):
         cols = slice(128 * g, 128 * g + 128)
-        fresh = q_recv[4 * g, 16:32, :].astype(F32)
-        for u in range(1, 4):
-            fresh += q_recv[4 * g + u, 16:32, :].astype(F32)
-        fresh_key = rotated(fresh, cosine, sine)[0:4].astype(BF16)
-        fresh_value = fresh[4:8].astype(BF16)
-        new_keys_ref[:, cols] = fresh_key
-        new_values_ref[:, cols] = fresh_value
+        fresh = n_recv[4 * g] + n_recv[4 * g + 1] + n_recv[4 * g + 2] + n_recv[4 * g + 3]
+        fresh = (fresh + low_f32[g]).astype(BF16)
+        fresh_key = rotated(fresh.astype(F32), cosine[0:8], sine[0:8])[0:4].astype(BF16)
+        fresh_value = fresh[4:8]
+        fresh_ref[0, :, cols] = fresh_key
+        fresh_ref[1, :, cols] = fresh_value
         pad = jnp.zeros((12, 128), BF16)
         k_buf[SLOTS : SLOTS + 16, cols] = jnp.concatenate([fresh_key, pad], 0)
         v_buf[SLOTS : SLOTS + 16, cols] = jnp.concatenate([fresh_value, pad], 0)
-        query = q_recv[4 * g : 4 * g + 4, 0:16, :].astype(F32).reshape(64, 128)
+        query = q_recv[4 * g : 4 * g + 4].astype(F32).reshape(64, 128)
         tables = (jnp.concatenate([cosine] * 4, 0), jnp.concatenate([sine] * 4, 0))
         query = rotated(query, *tables).astype(BF16)
         scores = scaling * lax.dot_general(
@@ -532,6 +558,7 @@
 
     def wait_q_sends(step, _):
         q_copy(step).wait_send()
+        n_copy(step).wait_send()
         return 0
 
     lax.fori_loop(1, 16, wait_q_sends, 0)
@@ -559,28 +586,19 @@
     hidden, w_query, w_key, w_value, a_factors, b_query, b_key, b_value,
     key_cache, value_cache, lengths,
 ):
-    half_dim = HEAD_DIM // 2
-    frequency = THETA ** (-(jnp.arange(half_dim, dtype=F32) * 2.0 / HEAD_DIM))
-    positions = lengths[0] + jnp.arange(16, dtype=jnp.int32) % STEPS
-    angles = positions.astype(F32)[:, None] * frequency
-    cosine, sine = jnp.cos(angles), jnp.sin(angles)
-    tables = jnp.stack(
-        [jnp.concatenate([cosine, cosine], 1), jnp.concatenate([-sine, sine], 1)]
-    )
-
     anywhere = pl.BlockSpec(memory_space=pltpu.HBM)
     vmem = pl.BlockSpec(memory_space=pltpu.VMEM)
     dma = pltpu.SemaphoreType.DMA
-    attended, new_keys, new_values = pl.pallas_call(
+    attended, fresh = pl.pallas_call(
         body,
         out_shape=(
             pltpu.VMEM((4, 16, 512), BF16),
-            pltpu.VMEM((4, 512), BF16),
-            pltpu.VMEM((4, 512), BF16),
+            pltpu.VMEM((2, 4, 512), BF16),
         ),
-        in_specs=[anywhere] * 11 + [vmem],
-        out_specs=(vmem, vmem, vmem),
+        in_specs=[anywhere] * 11,
+        out_specs=(vmem, vmem),
         scratch_shapes=[
+            pltpu.VMEM((2, 16, 128), F32),
             pltpu.SMEM((1,), jnp.int32),
             pltpu.VMEM((4, WIDTH), BF16),
             pltpu.VMEM((4, 512), BF16),
@@ -596,7 +614,7 @@
             pltpu.VMEM((32, 128), BF16),
             pltpu.VMEM((16, 32, 128), BF16),
             pltpu.VMEM((64, 512), BF16),
-            pltpu.VMEM((128, 128), BF16),
+            pltpu.VMEM((32, 128), BF16),
             pltpu.VMEM((2, 16, 1024), F32),
             pltpu.VMEM((16, 2, 16, 1024), BF16),
             pltpu.VMEM((16, WIDTH), F32),
@@ -606,13 +624,15 @@
             pltpu.VMEM((16, 16, 128), BF16),
             pltpu.VMEM((16, 8, 128), F32),
             pltpu.VMEM((16, 8, 128), F32),
-            pltpu.VMEM((16, 8, 128), F32),
-            pltpu.VMEM((64, 128), F32),
+            pltpu.VMEM((16, 32, 128), BF16),
+            pltpu.VMEM((4, 8, 128), F32),
             pltpu.VMEM((64, 512), F32),
             pltpu.VMEM((64, 64), F32),
-            pltpu.VMEM((16, 32, 128), F32),
-            pltpu.VMEM((16, 32, 128), BF16),
-            pltpu.VMEM((16, 32, 128), BF16),
+            pltpu.VMEM((16, 16, 128), F32),
+            pltpu.VMEM((16, 16, 128), BF16),
+            pltpu.VMEM((16, 16, 128), BF16),
+            pltpu.VMEM((16, 8, 128), F32),
+            pltpu.VMEM((16, 8, 128), F32),
             pltpu.VMEM((16, 16, 128), BF16),
             pltpu.VMEM((16, 16, 128), BF16),
             pltpu.VMEM((256, 128), F32),
@@ -620,6 +640,7 @@
             dma((3, 4)), dma((8,)), dma((8,)),
             dma((4,)), dma((4, 2)), dma((4, 2)), dma((16, 2)), dma((16,)), dma((16,)),
             dma((16,)), dma((16,)), dma((16,)), dma((16,)), dma((16,)), dma((16,)),
+            dma((16,)), dma((16,)),
             dma((16,)), dma((16,)), dma((16,)), dma((16,)),
         ],
         compiler_params=pltpu.CompilerParams(
@@ -628,9 +649,9 @@
     )(
         lengths, hidden[:, 0], w_query, w_key.T, w_value.T,
         jnp.swapaxes(a_factors, 1, 2).reshape(192, 512), b_query, b_key, b_value,
-        key_cache[0], value_cache[0], tables,
+        key_cache[0], value_cache[0],
     )
-    return attended, new_keys[:, None], new_values[:, None]
+    return attended, fresh[0][:, None], fresh[1][:, None]
 
 
 def solution(mesh):

time: 59.2 us -> 56.4 us (0.953)
  Pallas kernels: 55 us -> 53.7 us
  other arithmetic: 0.82 us -> 0 us
    pallas_call x1, Pallas kernels: 55 us -> 53.7 us  [shards(): pl.pallas_call(body, out_shape=(pltpu.VMEM((4, 16, 512), BF16), pltpu.VME...]
    unnamed x3 -> x1, local copies, waits for them, and re-layouts: 1.82 us -> 0.63 us
    another operation x2 -> x0, other arithmetic: 0.69 us -> none  [shards(): jnp.stack([jnp.concatenate([cosine, cosine], 1), jnp.concatenate([-sine,...]
    another operation x0 -> x1, local copies, waits for them, and re-layouts: none -> 0.6 us  [shards(): return (attended, fresh[0][:, None], fresh[1][:, None])]
where the time goes in v3:
time: 56.4 us; the launch traced here: 56.3 us
  Pallas kernels  53.7 us (95%)
  between operations  1.29 us (2%)
  local copies, waits for them, and re-layouts  1.23 us (2%)
    pallas_call x1, Pallas kernels, shards(): pl.pallas_call(body, out_shape=(pltpu.VMEM((4, 16, 512), BF16), pltpu.VME...  53.7 us

profile of v3, /device:TPU:1, one launch (start us, length us, event | category | flops | bytes accessed | tf_op | source)
XLA Modules:
  0.0 56.3 jit_solution(18076284477350990922)
XLA Ops:
  1.3 53.7 %shard_map.130 = (bf16[4,16,512]{2,1,0:T(8,128)(2,1)S(1)}, bf16[2,4,512]{2,1,0:T(4,128)(2,1)S(1)}) custom-call(s32[1]{0:T(128)S(6)} %copy.16.lengths_ref, bf16[4,8192]{1,0:T(4,128)(2,1)} %bitcast.17, bf16[8192,512]{1,0:T(8,128)(2,1)} %wq_ref.1, bf16[32,8192]{1,0:T(8,128)(2,1)} %bitcast.14, bf16[32,8192]{1,0:T(8,128)(2,1)} %bitcast.15, ...), custom_call_target="tpu_custom_call" | custom-call | tf_op jit(solution)/shard_map/pallas_call | solution.py:592
  55.0 0.6 %copy.15 = bf16[4,16,512]{2,1,0:T(8,128)(2,1)} copy(bf16[4,16,512]{2,1,0:T(8,128)(2,1)S(1)} %get-tuple-element.9) | data formatting | bytes 131072
  55.7 0.6 %slice_bitcast_fusion = (bf16[4,1,512]{2,0,1:T(4,128)(2,1)}, bf16[4,1,512]{2,0,1:T(4,128)(2,1)}) fusion(bf16[2,4,512]{2,1,0:T(4,128)(2,1)S(1)} %get-tuple-element.6), kind=kLoop, calls=%fused_computation | loop fusion | bytes 16384 | tf_op jit(solution)/shard_map/broadcast_in_dim;squeeze | solution.py:654

commit v4 on v3

--- a/solution.py
+++ b/solution.py
@@ -17,7 +17,7 @@
 BF16 = jnp.bfloat16
 
 SLOTS = 1536
-LAG, ES, EW, EH = 3, 6, 10, 15
+LAG, ES, EW, EH = 4, 8, 12, 15
 KEYS = SLOTS + 128
 WIDTH = 8192
 HALF = WIDTH // 2
@@ -503,12 +503,16 @@
         low = jnp.dot(totals, up_all, preferred_element_type=F32)
         low_f32[g] = jnp.where(key_row, low[0:8] + low[8:16], low[16:24] + low[24:32])
 
-    def wait_q(step, _):
-        q_copy(step).wait_recv()
-        n_copy(step).wait_recv()
-        return 0
-
-    lax.fori_loop(1, 16, wait_q, 0)
+    def wait_q(g, u, _):
+        step = (t + 16 - 4 * g - u) % 16
+
+        @pl.when(step != 0)
+        def _():
+            q_copy(step).wait_recv()
+            n_copy(step).wait_recv()
+
+        return 0
+
 
     cosine, sine = tables[0], tables[1]
     length = length_in[0]
@@ -524,11 +528,17 @@
         to = (t + step) % 16
         return remote(o_send.at[to], o_recv.at[t], o_ssem.at[step], o_rsem.at[step], (r, to))
 
-    def start_o(step, _):
-        o_copy(step).start()
+    def start_o(g, u, _):
+        step = (4 * g + u + 16 - t) % 16
+
+        @pl.when(step != 0)
+        def _():
+            o_copy(step).start()
+
         return 0
 
     for g in range(4):
+        lax.fori_loop(0, 4, functools.partial(wait_q, g), 0)
         cols = slice(128 * g, 128 * g + 128)
         fresh = n_recv[4 * g] + n_recv[4 * g + 1] + n_recv[4 * g + 2] + n_recv[4 * g + 3]
         fresh = (fresh + low_f32[g]).astype(BF16)
@@ -552,8 +562,8 @@
         probs = (weights * (1.0 / total)).astype(BF16)
         blended = jnp.dot(probs, v_buf[:, cols], preferred_element_type=F32).astype(BF16)
         o_send[4 * g : 4 * g + 4] = blended.reshape(4, 16, 128)
-
-    lax.fori_loop(1, 16, start_o, 0)
+        lax.fori_loop(0, 4, functools.partial(start_o, g), 0)
+
     o_recv[t] = o_send[t]
 
     def wait_q_sends(step, _):

time: 56.4 us -> 54.2 us (0.961)
  Pallas kernels: 53.7 us -> 51.6 us
    pallas_call x1, Pallas kernels: 53.7 us -> 51.6 us  [shards(): pl.pallas_call(body, out_shape=(pltpu.VMEM((4, 16, 512), BF16), pltpu.VME...]
where the time goes in v4:
time: 54.2 us; the launch traced here: 54.1 us
  Pallas kernels  51.6 us (95%)
  between operations  1.29 us (2%)
  local copies, waits for them, and re-layouts  1.23 us (2%)
    pallas_call x1, Pallas kernels, shards(): pl.pallas_call(body, out_shape=(pltpu.VMEM((4, 16, 512), BF16), pltpu.VME...  51.6 us

profile of v4, /device:TPU:1, one launch (start us, length us, event | category | flops | bytes accessed | tf_op | source)
XLA Modules:
  0.0 54.1 jit_solution(14609590801682153100)
XLA Ops:
  1.3 51.6 %shard_map.130 = (bf16[4,16,512]{2,1,0:T(8,128)(2,1)S(1)}, bf16[2,4,512]{2,1,0:T(4,128)(2,1)S(1)}) custom-call(s32[1]{0:T(128)S(6)} %copy.16.lengths_ref, bf16[4,8192]{1,0:T(4,128)(2,1)} %bitcast.17, bf16[8192,512]{1,0:T(8,128)(2,1)} %wq_ref.1, bf16[32,8192]{1,0:T(8,128)(2,1)} %bitcast.14, bf16[32,8192]{1,0:T(8,128)(2,1)} %bitcast.15, ...), custom_call_target="tpu_custom_call" | custom-call | tf_op jit(solution)/shard_map/pallas_call | solution.py:602
  52.9 0.6 %copy.15 = bf16[4,16,512]{2,1,0:T(8,128)(2,1)} copy(bf16[4,16,512]{2,1,0:T(8,128)(2,1)S(1)} %get-tuple-element.9) | data formatting | bytes 131072
  53.5 0.6 %slice_bitcast_fusion = (bf16[4,1,512]{2,0,1:T(4,128)(2,1)}, bf16[4,1,512]{2,0,1:T(4,128)(2,1)}) fusion(bf16[2,4,512]{2,1,0:T(4,128)(2,1)S(1)} %get-tuple-element.6), kind=kLoop, calls=%fused_computation | loop fusion | bytes 16384 | tf_op jit(solution)/shard_map/broadcast_in_dim;squeeze | solution.py:664
